TPU v7x, 512 devices: a whole 4x4x16 slice. The times are simulated.
512 devices in a mesh: aux: 64 (over x, z), pair: 8 (over y, core).
Axes of the slice: x: 4, y: 4, z: 16, core: 2. Of those that a mesh axis runs over, the one named last changes fastest.
Arguments:
- three_center: bfloat16 [512, 64, 1024], P('aux', 'pair'), may hold values from -6 to 6
- tile_live: int32 [64, 64], P('aux', 'pair'), may hold values from 0 to 1
- pair_atoms: int32 [64], replicated, may hold values from 0 to 63, each once
- green_occ: bfloat16 [256, 256], replicated, may hold values from -0.375 to 0.375
- green_vir: bfloat16 [256, 256], replicated, may hold values from -0.375 to 0.375
- screened: bfloat16 [512, 40], P('aux'), may hold values from -1 to 1
Outputs:
- polarizability: float32 [512, 40], P('aux', 'pair')
- self_energy: float32 [64, 1024], P('pair')
Inputs may be any that keep to these rules, and one draw needn't show every extreme that they name: `pair_atoms`: a permutation of the 64 atom pairs.
All inputs are finite; a program needn't handle non-finite values.
Results may differ from a plain program's by a relative error of at most 0.0043.
Values may be sent and summed in bfloat16 or wider, within the bound.
A program may use at most 64 MiB of HBM per device.

v0:
```python
import math

import jax
import jax.numpy as jnp
from jax import lax
from jax.sharding import PartitionSpec as P

OA = 32
NAT = 8
REACH = 2


def shifted(value, axis, steps):
    count = lax.axis_size(axis)
    initial, last = (max(0, -steps), min(count, count - steps))
    return lax.ppermute(value, axis, [(source, source + steps) for source in range(initial, last)])


def side_by_side(arrays, axis, split_dim, concat_dim, along):
    ends, at = ([], 0)
    for a in arrays[:-1]:
        at += a.shape[along]
        ends.append(at)
    both = jnp.concatenate(arrays, axis=along)
    return tuple(
        jnp.split(
            lax.all_to_all(both, axis, split_axis=split_dim, concat_axis=concat_dim, tiled=True),
            ends,
            axis=along,
        )
    )


def in_blocks(array, dim, peers):
    before, after = (array.shape[:dim], array.shape[dim + 1 :])
    return jnp.moveaxis(array.reshape(*before, peers, -1, *after), dim, 0)


def summed_on_arrival(array, axis, dim):
    peers = lax.axis_size(axis)
    blocks = lax.all_to_all(in_blocks(array, dim, peers), axis, 0, 0, tiled=True)
    return jnp.sum(blocks, axis=0)


def from_everyone(array, axis):
    peers = lax.axis_size(axis)
    return lax.all_to_all(
        jnp.broadcast_to(array[None], (peers, *array.shape)), axis, 0, 0, tiled=True
    )


def joined_along(blocks, dim):
    shape = list(blocks.shape[1:])
    shape[dim] *= blocks.shape[0]
    return jnp.moveaxis(blocks, 0, dim).reshape(shape)


def gather_directly(array, axis, dim):
    blocks = from_everyone(array, axis)
    return joined_along(blocks, dim)


def tiles_to_matrix(tile_data, inverse):
    tile_rows = tile_data.shape[0]
    ordered = jnp.take(tile_data, inverse, axis=1)
    reshaped = ordered.reshape(tile_rows, NAT, NAT, OA, OA)
    return jnp.transpose(reshaped, (0, 1, 3, 2, 4)).reshape(tile_rows, NAT * OA, NAT * OA)


def matrix_to_tiles(matrix, pair_atoms):
    tile_rows = matrix.shape[0]
    reshaped = matrix.reshape(tile_rows, NAT, OA, NAT, OA)
    ordered = jnp.transpose(reshaped, (0, 1, 3, 2, 4)).reshape(tile_rows, NAT * NAT, OA * OA)
    return jnp.take(ordered, pair_atoms, axis=1)


def neighbor_window(masked):
    pieces = []
    for offset in range(-REACH, REACH + 1):
        if offset == 0:
            pieces.append(masked)
        else:
            pieces.append(shifted(masked, "aux", -offset))
    return jnp.concatenate(pieces, axis=0)


def row_groups(orbital_form, group_fn):
    row_count = orbital_form.shape[0]
    group_size = math.gcd(row_count, 8)
    grouped = orbital_form.reshape(row_count // group_size, group_size, NAT * OA, NAT * OA)
    result = lax.map(group_fn, grouped)
    return result.reshape((row_count,) + result.shape[2:])


def all_products(orbital_form, green_occ, green_vir):

    def group_fn(row_group):
        left_half = jnp.einsum(
            "lu,plm->pum", green_occ, row_group, preferred_element_type=jnp.float32
        ).astype(jnp.bfloat16)
        return jnp.einsum(
            "pum,mv->puv", left_half, green_vir, preferred_element_type=jnp.float32
        ).astype(jnp.bfloat16)

    return row_groups(orbital_form, group_fn)


def energy_rows(mixed_tiles, occ_rows, orbital_form, tile_first):
    tile_rows, tile_count = (mixed_tiles.shape[0], mixed_tiles.shape[1])
    mixed_tiles = mixed_tiles.reshape(tile_rows, tile_count, OA, OA)
    scaled_rows = jnp.einsum(
        "qkml,kls->qkms", mixed_tiles, occ_rows, preferred_element_type=jnp.float32
    ).astype(jnp.bfloat16)
    term_sums = jnp.einsum(
        "qkms,qsn->kmn", scaled_rows, orbital_form, preferred_element_type=jnp.float32
    )
    atom_onehot = (tile_first[:, None] == jnp.arange(NAT, dtype=jnp.int32)[None, :]).astype(
        jnp.float32
    )
    return jnp.einsum("ka,kmn->amn", atom_onehot, term_sums, precision=lax.Precision.HIGHEST)


def per_device(three_center, tile_live, pair_atoms, green_occ, green_vir, screened):
    row_count, own_count = (three_center.shape[0], three_center.shape[1])
    masked = three_center * tile_live[0].astype(jnp.bfloat16)[:, None]
    inverse = jnp.argsort(pair_atoms)
    first_atom = pair_atoms // NAT
    second_atom = pair_atoms % NAT
    occ_rows = green_occ.reshape(NAT, OA, NAT * OA)
    window = neighbor_window(masked)
    flat_window = window.reshape(window.shape[0], own_count * OA * OA)
    mixed_tiles = jnp.dot(screened, flat_window, preferred_element_type=jnp.float32).astype(
        jnp.bfloat16
    )
    mixed_tiles = mixed_tiles.reshape(row_count, own_count, OA * OA)
    sub_tiles, sub_mixed = side_by_side((masked, mixed_tiles), "pair", 0, 1, 2)
    orbital_form = tiles_to_matrix(sub_tiles, inverse)
    full_form = all_products(orbital_form, green_occ, green_vir)
    products = lax.all_to_all(
        matrix_to_tiles(full_form, pair_atoms), "pair", split_axis=1, concat_axis=0, tiled=True
    )
    by_atom = energy_rows(
        sub_mixed, jnp.take(occ_rows, second_atom, axis=0), orbital_form, first_atom
    )
    chi_part = lax.dot_general(
        products.reshape(row_count, own_count * OA * OA),
        flat_window,
        (((1,), (1,)), ((), ())),
        preferred_element_type=jnp.float32,
    ) * (1.0 / (OA * NAT))
    polarizability = summed_on_arrival(chi_part, "pair", 1)
    aux_total = row_count * lax.axis_size("aux")
    sigma_scale = 1.0 / math.sqrt(aux_total * NAT * OA * NAT)
    partial_value = (
        matrix_to_tiles(by_atom.reshape(1, NAT * OA, NAT * OA), pair_atoms)[0] * -sigma_scale
    )
    columns = summed_on_arrival(partial_value, "aux", 1)
    owned_tiles = summed_on_arrival(columns, "pair", 0)
    self_energy = gather_directly(owned_tiles, "aux", 1)
    return (polarizability, self_energy)


def solution(mesh):
    placed = (P("aux", "pair", None), P("aux", "pair"), P(), P(), P(), P("aux", None))
    return jax.shard_map(
        per_device,
        mesh=mesh,
        in_specs=placed,
        out_specs=(P("aux", "pair"), P("pair", None)),
        check_vma=False,
    )
```

profile of v0, /device:TPU:1, one launch (start us, length us, event | category | flops | bytes accessed | tf_op | source)
XLA Modules:
  0.0 136.3 jit_solution(14606263857130700433)
XLA Ops:
  0.7 0.7 convert_bitcast_fusion
  1.4 1.0 broadcast_multiply_fusion
  2.3 5.7 %collective-permute-start = (bf16[8,8,1024]{2,1,0:T(8,128)(2,1)S(1)}, bf16[8,8,1024]{2,1,0:T(8,128)(2,1)S(1)}, u32[]{:S(2)}, u32[]{:S(2)}) collective-permute-start(bf16[8,8,1024]{2,1,0:T(8,128)(2,1)S(1)} %broadcast_multiply_fusion), channel_id=1, source_target_pairs={{0,16},{8,24},{16,32},{24,40},{32,48},{40,56},{48,64},{56,72},{64,... | collective-permute-start | bytes 393224 | tf_op jit(solution)/shard_map/ppermute | solution.py:16
  8.1 3.5 %collective-permute-start.1 = (bf16[8,8,1024]{2,1,0:T(8,128)(2,1)S(1)}, bf16[8,8,1024]{2,1,0:T(8,128)(2,1)S(1)}, u32[]{:S(2)}, u32[]{:S(2)}) collective-permute-start(bf16[8,8,1024]{2,1,0:T(8,128)(2,1)S(1)} %broadcast_multiply_fusion), channel_id=1, source_target_pairs={{0,8},{8,16},{16,24},{24,32},{32,40},{40,48},{48,56},{56,64},{64,7... | collective-permute-start | bytes 393224 | tf_op jit(solution)/shard_map/ppermute | solution.py:16
  11.6 1.3 collective-permute-start.2
  12.9 1.3 collective-permute-start.3
  14.2 0.7 compare_and_fusion.2
  14.9 0.7 and_select_fusion.1
  15.6 2.7 %sort.17 = (s32[64]{0:T(128)}, s32[64]{0:T(128)S(1)}) sort(s32[64]{0:T(128)} %param.10, s32[64]{0:T(128)S(1)} %iota.8), dimensions={0}, to_apply=%region_0.0 | sort | flops 384 | bytes 1024 | tf_op jit(solution)/shard_map/jit(argsort)/sort | solution.py:126
  18.3 1.0 constant_dynamic-update-slice_fusion.2
  19.4 6.0 %collective-permute-done.3 = bf16[8,8,1024]{2,1,0:T(8,128)(2,1)S(1)} collective-permute-done((bf16[8,8,1024]{2,1,0:T(8,128)(2,1)S(1)}, bf16[8,8,1024]{2,1,0:T(8,128)(2,1)S(1)}, u32[]{:S(2)}, u32[]{:S(2)}) %collective-permute-start.3) | collective-permute-done | bytes 131104 | tf_op jit(solution)/shard_map/ppermute | solution.py:16
  25.4 0.4 copy.41
  25.8 0.2 convolution_convert_fusion
  26.1 0.7 pad_maximum_fusion
  26.8 7.0 %all-to-all-start = ((bf16[8,8,2048]{2,1,0:T(8,128)(2,1)}), bf16[8,8,2048]{2,1,0:T(8,128)(2,1)S(1)}, u32[]{:S(2)}, u32[]{:S(2)}) async-start(bf16[8,8,2048]{2,1,0:T(8,128)(2,1)} %pad_maximum_fusion), calls=%async_computation | async-start | bytes 524288 | tf_op jit(solution)/shard_map/all_to_all | solution.py:27
  33.8 0.6 gather_fusion
  34.4 5.8 %all-to-all-done = bf16[8,8,2048]{2,1,0:T(8,128)(2,1)S(1)} async-done(((bf16[8,8,2048]{2,1,0:T(8,128)(2,1)}), bf16[8,8,2048]{2,1,0:T(8,128)(2,1)S(1)}, u32[]{:S(2)}, u32[]{:S(2)}) %all-to-all-start) | async-done | bytes 262176 | tf_op jit(solution)/shard_map/all_to_all | solution.py:27
  40.3 0.7 gather_fusion.2
  41.1 0.4 reshape.130
  41.5 0.2 copy.46
  41.7 0.3 reshape.131
  42.1 0.4 reshape.194
  42.4 0.5 convolution_convert_fusion.2
  42.9 0.2 reshape_reshape.7
  43.2 0.5 reshape.190
  43.8 0.7 gather_fusion.3
  44.6 0.2 copy.47
  44.8 0.5 broadcast.66
  45.3 1.4 %reduce.2 = bf16[64,1024]{1,0:T(8,128)(2,1)S(1)} reduce(bf16[64,1,1024]{2,1,0:T(2,128)(2,1)S(1)} %bitcast.84, bf16[]{:T(256)} %broadcast.66), dimensions={1}, to_apply=%bitcast.74.reduce_sub_computation | reduce | bytes 262146
  46.7 0.7 reshape.199
  47.4 4.3 %all-to-all-start.1 = ((bf16[8,2,4096]{2,1,0:T(2,128)(2,1)}), bf16[8,2,4096]{2,1,0:T(2,128)(2,1)S(1)}, u32[]{:S(2)}, u32[]{:S(2)}) async-start(bf16[8,2,4096]{2,1,0:T(2,128)(2,1)} %reshape.199), calls=%async_computation.1 | async-start | bytes 262144 | tf_op jit(solution)/shard_map/all_to_all | solution.py:139
  51.7 0.2 copy.34
  51.9 0.8 copy.35
  52.7 0.5 fusion
  53.2 1.3 fusion.2
  54.5 0.8 fusion.8
  55.2 0.3 reshape_reshape.8
  55.5 0.6 copy.37
  56.1 0.5 reshape.170
  56.6 0.7 gather_fusion.1
  57.3 0.2 copy.38
  57.6 1.0 reshape.201
  58.6 14.4 %all-to-all-start.3 = ((f32[64,1,1024]{2,1,0:T(1,128)}), f32[64,1,1024]{2,1,0:T(1,128)S(1)}, u32[]{:S(2)}, u32[]{:S(2)}) async-start(f32[64,1,1024]{2,1,0:T(1,128)} %reshape.201), calls=%async_computation.3 | async-start | bytes 524288 | tf_op jit(solution)/shard_map/all_to_all | solution.py:41
  73.0 0.1 reshape.200
  73.2 0.7 bitcast_reduce_fusion.1
  74.0 19.1 %all-to-all-done.3 = f32[64,1,1024]{2,1,0:T(1,128)S(1)} async-done(((f32[64,1,1024]{2,1,0:T(1,128)}), f32[64,1,1024]{2,1,0:T(1,128)S(1)}, u32[]{:S(2)}, u32[]{:S(2)}) %all-to-all-start.3) | async-done | bytes 262176 | tf_op jit(solution)/shard_map/all_to_all | solution.py:41
  93.0 0.5 broadcast.67
  93.6 1.3 reduce.3
  94.8 0.1 reshape.202
  95.1 0.7 reshape.203
  95.8 6.2 %all-to-all-start.4 = ((f32[8,1,128]{2,1,0:T(1,128)}), f32[8,1,128]{2,1,0:T(1,128)S(1)}, u32[]{:S(2)}, u32[]{:S(2)}) async-start(f32[8,1,128]{2,1,0:T(1,128)} %reshape.203), calls=%async_computation.4 | async-start | bytes 8192 | tf_op jit(solution)/shard_map/all_to_all | solution.py:41
  102.0 0.3 convolution_multiply_fusion
  102.4 0.6 copy.33
  103.0 3.5 %all-to-all-done.4 = f32[8,1,128]{2,1,0:T(1,128)S(1)} async-done(((f32[8,1,128]{2,1,0:T(1,128)}), f32[8,1,128]{2,1,0:T(1,128)S(1)}, u32[]{:S(2)}, u32[]{:S(2)}) %all-to-all-start.4) | async-done | bytes 4128 | tf_op jit(solution)/shard_map/all_to_all | solution.py:41
  106.5 3.9 %all-to-all-start.2 = ((f32[8,8,5]{2,1,0:T(8,128)}), f32[8,8,5]{2,1,0:T(8,128)S(1)}, u32[]{:S(2)}, u32[]{:S(2)}) async-start(f32[8,8,5]{2,1,0:T(8,128)} %copy.33), calls=%async_computation.2 | async-start | bytes 65536 | tf_op jit(solution)/shard_map/all_to_all | solution.py:41
  110.5 0.6 reduce.4
  111.2 0.8 reshape.205
  112.0 3.2 %all-to-all-done.2 = f32[8,8,5]{2,1,0:T(8,128)S(1)} async-done(((f32[8,8,5]{2,1,0:T(8,128)}), f32[8,8,5]{2,1,0:T(8,128)S(1)}, u32[]{:S(2)}, u32[]{:S(2)}) %all-to-all-start.2) | async-done | bytes 1312 | tf_op jit(solution)/shard_map/all_to_all | solution.py:41
  115.2 6.2 %all-to-all-start.5 = ((f32[64,1,128]{2,1,0:T(1,128)}), f32[64,1,128]{2,1,0:T(1,128)S(1)}, u32[]{:S(2)}, u32[]{:S(2)}) async-start(f32[64,1,128]{2,1,0:T(1,128)} %reshape.205), calls=%async_computation.5 | async-start | bytes 65536 | tf_op jit(solution)/shard_map/all_to_all | solution.py:47
  121.4 0.6 reduce_sum.27
  122.0 12.7 %all-to-all-done.5 = f32[64,1,128]{2,1,0:T(1,128)S(1)} async-done(((f32[64,1,128]{2,1,0:T(1,128)}), f32[64,1,128]{2,1,0:T(1,128)S(1)}, u32[]{:S(2)}, u32[]{:S(2)}) %all-to-all-start.5) | async-done | bytes 32800 | tf_op jit(solution)/shard_map/all_to_all | solution.py:47
  134.7 0.7 reduce.5
  135.4 0.1 reshape.206
  135.6 0.8 reshape.141
  (33 shorter events, 1.0 us)
Async XLA Ops:
  0.6 33.2 %copy-start = (bf16[256,256]{1,0:T(8,128)(2,1)S(1)}, bf16[256,256]{1,0:T(8,128)(2,1)}, u32[]{:S(2)}) copy-start(bf16[256,256]{1,0:T(8,128)(2,1)} %param.11) | copy-start | bytes 393220
  0.6 25.2 %copy-start.1 = (bf16[8,40]{1,0:T(8,128)(2,1)S(1)}, bf16[8,40]{1,0:T(8,128)(2,1)}, u32[]{:S(2)}) copy-start(bf16[8,40]{1,0:T(8,128)(2,1)} %param.13) | copy-start | bytes 1924
  2.3 15.9 %collective-permute-start = (bf16[8,8,1024]{2,1,0:T(8,128)(2,1)S(1)}, bf16[8,8,1024]{2,1,0:T(8,128)(2,1)S(1)}, u32[]{:S(2)}, u32[]{:S(2)}) collective-permute-start(bf16[8,8,1024]{2,1,0:T(8,128)(2,1)S(1)} %broadcast_multiply_fusion), channel_id=1, source_target_pairs={{0,16},{8,24},{16,32},{24,40},{32,48},{40,56},{48,64},{56,72},{64,... | collective-permute-start | bytes 393224 | tf_op jit(solution)/shard_map/ppermute | solution.py:16
  8.1 10.2 %collective-permute-start.1 = (bf16[8,8,1024]{2,1,0:T(8,128)(2,1)S(1)}, bf16[8,8,1024]{2,1,0:T(8,128)(2,1)S(1)}, u32[]{:S(2)}, u32[]{:S(2)}) collective-permute-start(bf16[8,8,1024]{2,1,0:T(8,128)(2,1)S(1)} %broadcast_multiply_fusion), channel_id=1, source_target_pairs={{0,8},{8,16},{16,24},{24,32},{32,40},{40,48},{48,56},{56,64},{64,7... | collective-permute-start | bytes 393224 | tf_op jit(solution)/shard_map/ppermute | solution.py:16
  11.6 7.7 %collective-permute-start.2 = (bf16[8,8,1024]{2,1,0:T(8,128)(2,1)S(1)}, bf16[8,8,1024]{2,1,0:T(8,128)(2,1)S(1)}, u32[]{:S(2)}, u32[]{:S(2)}) collective-permute-start(bf16[8,8,1024]{2,1,0:T(8,128)(2,1)S(1)} %broadcast_multiply_fusion), channel_id=1, source_target_pairs={{8,0},{16,8},{24,16},{32,24},{40,32},{48,40},{56,48},{64,56},{72,6... | collective-permute-start | bytes 393224 | tf_op jit(solution)/shard_map/ppermute | solution.py:16
  12.9 12.5 %collective-permute-start.3 = (bf16[8,8,1024]{2,1,0:T(8,128)(2,1)S(1)}, bf16[8,8,1024]{2,1,0:T(8,128)(2,1)S(1)}, u32[]{:S(2)}, u32[]{:S(2)}) collective-permute-start(bf16[8,8,1024]{2,1,0:T(8,128)(2,1)S(1)} %broadcast_multiply_fusion), channel_id=1, source_target_pairs={{16,0},{24,8},{32,16},{40,24},{48,32},{56,40},{64,48},{72,56},{80,... | collective-permute-start | bytes 393224 | tf_op jit(solution)/shard_map/ppermute | solution.py:16
  26.8 13.5 %all-to-all-start = ((bf16[8,8,2048]{2,1,0:T(8,128)(2,1)}), bf16[8,8,2048]{2,1,0:T(8,128)(2,1)S(1)}, u32[]{:S(2)}, u32[]{:S(2)}) async-start(bf16[8,8,2048]{2,1,0:T(8,128)(2,1)} %pad_maximum_fusion), calls=%async_computation | async-start | bytes 524288 | tf_op jit(solution)/shard_map/all_to_all | solution.py:27
  40.3 2.1 %copy-start.2 = (bf16[256,256]{1,0:T(8,128)(2,1)S(1)}, bf16[256,256]{1,0:T(8,128)(2,1)}, u32[]{:S(2)}) copy-start(bf16[256,256]{1,0:T(8,128)(2,1)} %param.12) | copy-start | bytes 393220
  47.4 11.2 %all-to-all-start.1 = ((bf16[8,2,4096]{2,1,0:T(2,128)(2,1)}), bf16[8,2,4096]{2,1,0:T(2,128)(2,1)S(1)}, u32[]{:S(2)}, u32[]{:S(2)}) async-start(bf16[8,2,4096]{2,1,0:T(2,128)(2,1)} %reshape.199), calls=%async_computation.1 | async-start | bytes 262144 | tf_op jit(solution)/shard_map/all_to_all | solution.py:139
  58.6 34.4 %all-to-all-start.3 = ((f32[64,1,1024]{2,1,0:T(1,128)}), f32[64,1,1024]{2,1,0:T(1,128)S(1)}, u32[]{:S(2)}, u32[]{:S(2)}) async-start(f32[64,1,1024]{2,1,0:T(1,128)} %reshape.201), calls=%async_computation.3 | async-start | bytes 524288 | tf_op jit(solution)/shard_map/all_to_all | solution.py:41
  95.8 10.7 %all-to-all-start.4 = ((f32[8,1,128]{2,1,0:T(1,128)}), f32[8,1,128]{2,1,0:T(1,128)S(1)}, u32[]{:S(2)}, u32[]{:S(2)}) async-start(f32[8,1,128]{2,1,0:T(1,128)} %reshape.203), calls=%async_computation.4 | async-start | bytes 8192 | tf_op jit(solution)/shard_map/all_to_all | solution.py:41
  106.5 8.7 %all-to-all-start.2 = ((f32[8,8,5]{2,1,0:T(8,128)}), f32[8,8,5]{2,1,0:T(8,128)S(1)}, u32[]{:S(2)}, u32[]{:S(2)}) async-start(f32[8,8,5]{2,1,0:T(8,128)} %copy.33), calls=%async_computation.2 | async-start | bytes 65536 | tf_op jit(solution)/shard_map/all_to_all | solution.py:41
  115.2 19.5 %all-to-all-start.5 = ((f32[64,1,128]{2,1,0:T(1,128)}), f32[64,1,128]{2,1,0:T(1,128)S(1)}, u32[]{:S(2)}, u32[]{:S(2)}) async-start(f32[64,1,128]{2,1,0:T(1,128)} %reshape.205), calls=%async_computation.5 | async-start | bytes 65536 | tf_op jit(solution)/shard_map/all_to_all | solution.py:47
where the time goes:
time: 137 us; the launch traced here: 136 us
  starting transfers between devices  53.9 us (39%)
  waiting for transfers between devices  50.4 us (37%)
  local copies, waits for them, and re-layouts  15.2 us (11%)
  other arithmetic  12.3 us (9%)
  matrix products  3.47 us (3%)
    all_to_all x3, waiting for transfers between devices, summed_on_arrival(): lax.all_to_all(in_blocks(array, dim, peers), axis, 0, 0, tiled=True)  25.8 us
    all_to_all x3, starting transfers between devices, summed_on_arrival(): lax.all_to_all(in_blocks(array, dim, peers), axis, 0, 0, tiled=True)  24.6 us
    all_to_all x1, waiting for transfers between devices, from_everyone(): lax.all_to_all(jnp.broadcast_to(array[None], (peers, *array.shape)), axis...  12.7 us
    ppermute x4, starting transfers between devices, shifted(): lax.ppermute(value, axis, [(source, source + steps) for source in range(i...  11.9 us
    all_to_all x1, starting transfers between devices, side_by_side(): lax.all_to_all(both, axis, split_axis=split_dim, concat_axis=concat_dim,...  6.97 us
    all_to_all x1, starting transfers between devices, from_everyone(): lax.all_to_all(jnp.broadcast_to(array[None], (peers, *array.shape)), axis...  6.15 us
    ppermute x4, waiting for transfers between devices, shifted(): lax.ppermute(value, axis, [(source, source + steps) for source in range(i...  6.05 us
    all_to_all x1, waiting for transfers between devices, side_by_side(): lax.all_to_all(both, axis, split_axis=split_dim, concat_axis=concat_dim,...  5.85 us
  transfers between devices with their start and end apart: 10, of which 6 were waited for; matrix products, arithmetic and copies ran while one was open for 12% of the time, Pallas kernels for 0%

commit v1 on v0

v1 whole, which is shorter than its diff:
```python
import functools
import math

import jax
import jax.numpy as jnp
from jax import lax
from jax.experimental import pallas as pl
from jax.experimental.pallas import tpu as pltpu
from jax.sharding import PartitionSpec as P

MESH = pl.DeviceIdType.MESH
OA = 32
NAT = 8
REACH = 2
NX = 4
NZ = 16
F32 = jnp.float32
BF16 = jnp.bfloat16


def dot(a, b, dims=((1,), (0,))):
    return lax.dot_general(a, b, (dims, ((), ())), preferred_element_type=F32)


def iota(shape, dim):
    return lax.broadcasted_iota(jnp.int32, shape, dim)


def exchange_groups(parts):
    x0, x1, x2, x3 = parts
    lane = iota(x0.shape, 1)
    low = lane < 64
    even = (lane & 32) == 0
    y0 = jnp.where(low, x0, pltpu.roll(x2, 64, 1))
    y2 = jnp.where(low, pltpu.roll(x0, 64, 1), x2)
    y1 = jnp.where(low, x1, pltpu.roll(x3, 64, 1))
    y3 = jnp.where(low, pltpu.roll(x1, 64, 1), x3)
    z0 = jnp.where(even, y0, pltpu.roll(y1, 32, 1))
    z1 = jnp.where(even, pltpu.roll(y0, 96, 1), y1)
    z2 = jnp.where(even, y2, pltpu.roll(y3, 32, 1))
    z3 = jnp.where(even, pltpu.roll(y2, 96, 1), y3)
    return z0, z1, z2, z3


def to_matrix(tiles):
    cols = [tiles[:, g * 128 : (g + 1) * 128].reshape(2, 4, 8, 128) for g in range(8)]
    parts = [
        jnp.concatenate([c[:, bl] for c in cols], axis=0).reshape(128, 128) for bl in range(4)
    ]
    out = [z.reshape(8, 2, 8, 128) for z in exchange_groups(parts)]
    halves = [
        jnp.stack([z[:, bh] for z in out], axis=1).reshape(256, 128) for bh in range(2)
    ]
    return jnp.concatenate(halves, axis=1)


def to_tiles(matrix):
    halves = [matrix[:, bh * 128 : (bh + 1) * 128].reshape(8, 4, 8, 128) for bh in range(2)]
    parts = [
        jnp.stack([h[:, r] for h in halves], axis=1).reshape(128, 128) for r in range(4)
    ]
    out = [z.reshape(8, 2, 8, 128) for z in exchange_groups(parts)]
    cols = [
        jnp.stack([z[g] for z in out], axis=1).reshape(64, 128) for g in range(8)
    ]
    return jnp.concatenate(cols, axis=1)


def rows64(value):
    return value.astype(F32).reshape(64, value.shape[-1])


def kernel(
    n_aux,
    n_pair,
    tc_hbm,
    live_hbm,
    atoms_hbm,
    occ_hbm,
    vir_hbm,
    scr_hbm,
    pol_ref,
    self_ref,
    tc,
    live,
    atoms,
    occ,
    vir,
    scr,
    win,
    mt,
    zo,
    zt,
    vo,
    vt,
    xo,
    xr,
    chi,
    yo,
    yr,
    ar,
    fin,
    in_sem,
    s_win,
    r_win,
    s_m,
    r_m,
    s_z,
    r_z,
    s_v,
    r_v,
    s_x,
    r_x,
    s_c,
    r_c,
    s_y,
    r_y,
    s_a,
    r_a,
    s_f,
    r_f,
):
    a_me = lax.axis_index("aux")
    p_me = lax.axis_index("pair")
    x_me, z_me = a_me // NZ, a_me % NZ
    zh_me, par_me = z_me // 2, z_me % 2
    j_me = x_me * 2 + par_me

    loads = [
        pltpu.make_async_copy(src, dst, in_sem.at[i])
        for i, (src, dst) in enumerate(
            (
                (tc_hbm, tc),
                (live_hbm, live),
                (atoms_hbm, atoms),
                (occ_hbm, occ),
                (vir_hbm, vir),
                (scr_hbm, scr),
            )
        )
    ]
    for c in loads:
        c.start()

    def by_pair(step):
        q = lax.rem(p_me + step, n_pair)
        return q, (a_me, q)

    def by_group(step):
        j = lax.rem(j_me + step, 8)
        return j, ((j // 2) * NZ + zh_me * 2 + lax.rem(j, 2), p_me)

    def by_zh(step):
        h = lax.rem(zh_me + step, 8)
        return h, (x_me * NZ + h * 2 + par_me, p_me)

    offsets = (1, -1, 2, -2)

    def by_window(d):
        return (lax.rem(a_me + d + n_aux, n_aux), p_me)

    barrier = pltpu.get_barrier_semaphore()
    for d in offsets:
        pl.semaphore_signal(barrier, inc=1, device_id=by_window(d), device_id_type=MESH)
    for step in range(1, 8):
        for peer in (by_pair, by_group, by_zh):
            pl.semaphore_signal(barrier, inc=1, device_id=peer(step)[1], device_id_type=MESH)

    def remote(src, dst, send, recv, device):
        return pltpu.make_async_remote_copy(
            src_ref=src,
            dst_ref=dst,
            send_sem=send,
            recv_sem=recv,
            device_id=device,
            device_id_type=MESH,
        )

    def exchange(peer, me, source, dest, send, recv):
        copies = []
        for step in range(1, 8):
            there, device = peer(step)
            src = source(there)
            copies.append(remote(src, dest.at[me], send.at[step - 1], recv.at[step - 1], device))
        for c in copies:
            c.start()
        return copies

    loads[0].wait()
    loads[1].wait()
    eye8 = iota((8, 8), 0) == iota((8, 8), 1)
    live_col = jnp.sum(
        jnp.where(eye8, jnp.broadcast_to(live[...].astype(F32), (8, 8)), 0.0), axis=1, keepdims=True
    )
    win[REACH] = (tc[...].astype(F32) * live_col[None]).astype(BF16)

    pl.semaphore_wait(barrier, 25)
    started = []
    window_copies = {}
    for i, d in enumerate(offsets):
        c = remote(win.at[REACH], win.at[REACH - d], s_win.at[i], r_win.at[i], by_window(d))
        c.start()
        window_copies[REACH - d] = c
        started.append(c)
    m_copies = exchange(by_pair, p_me, lambda q: win.at[REACH, q], mt, s_m, r_m)
    started += m_copies
    mt[p_me] = win[REACH, p_me]

    for c in loads[2:]:
        c.wait()
    new = iota((256, 256), 0)
    old = iota((256, 256), 1)
    perm = jnp.where((new % 8) * 32 + new // 8 == old, 1.0, 0.0).astype(BF16)
    occ_cols = dot(occ[...], perm, ((1,), (1,))).astype(BF16)
    occ_both = dot(perm, occ_cols).astype(BF16)
    atom_row = atoms[...]
    place = iota((64, 64), 0)
    pick = jnp.where((place % 8) * 8 + place // 8 == atom_row, 1.0, 0.0).astype(BF16)
    eye64 = iota((64, 64), 0) == iota((64, 64), 1)
    atom_col = jnp.sum(
        jnp.where(eye64, jnp.broadcast_to(atom_row.astype(F32), (64, 64)), 0.0), axis=1, keepdims=True
    ).astype(jnp.int32)
    spot = iota((64, 64), 1)
    put = jnp.where((spot % 8) * 8 + spot // 8 == atom_col, 1.0, 0.0).astype(BF16)
    wide = jnp.broadcast_to(scr[...].astype(F32)[:, None, :], (8, 8, 40)).reshape(64, 40).astype(BF16)
    same_tile = (iota((64, 64), 0) % 8) == (iota((64, 64), 1) % 8)
    couple = []
    for slot in range(5):
        spread = jnp.where(iota((40, 64), 0) == slot * 8 + iota((40, 64), 1) // 8, 1.0, 0.0)
        block = a_me + slot - REACH
        inside = jnp.logical_and(block >= 0, block < n_aux)
        keep = jnp.logical_and(same_tile, inside)
        couple.append(jnp.where(keep, dot(wide, spread.astype(BF16)), 0.0).astype(BF16))

    for c in m_copies:
        c.wait_recv()
    form = to_matrix(dot(pick, rows64(mt[...]).astype(BF16))).astype(BF16)
    left = dot(occ_both, form, ((0,), (0,))).astype(BF16)
    product = dot(left, vir[...])
    z_tiles = dot(put, to_tiles(product).astype(BF16))
    zo[...] = z_tiles.reshape(8, 8, 1024).astype(BF16)
    z_copies = exchange(by_pair, p_me, lambda q: zo.at[q], zt, s_z, r_z)
    started += z_copies
    zt[p_me] = zo[p_me]

    mixed = dot(couple[2], rows64(win[2]).astype(BF16))
    for slot in (1, 3, 0, 4):
        window_copies[slot].wait_recv()
        mixed += dot(couple[slot], rows64(win[slot]).astype(BF16))
    vo[...] = mixed.reshape(8, 8, 1024).astype(BF16)
    v_copies = exchange(by_pair, p_me, lambda q: vo.at[q], vt, s_v, r_v)
    started += v_copies
    vt[p_me] = vo[p_me]

    for c in z_copies:
        c.wait_recv()
    z_rows = rows64(zt[...]).astype(BF16)
    chi_total = jnp.zeros((8, 128), F32)
    for slot in range(5):
        terms = dot(z_rows, rows64(win[slot]).astype(BF16), ((1,), (1,)))
        block = a_me + slot - REACH
        inside = jnp.logical_and(block >= 0, block < n_aux)
        keep = jnp.logical_and(same_tile, inside)
        terms = jnp.sum(jnp.where(keep, terms, 0.0).reshape(8, 8, 64), axis=1)
        gather = jnp.where(iota((64, 128), 1) == slot * 8 + iota((64, 128), 0) // 8, 1.0, 0.0)
        chi_total += jnp.dot(terms, gather, precision=lax.Precision.HIGHEST, preferred_element_type=F32)
    chi[p_me] = chi_total * (1.0 / (OA * NAT))
    c_copies = exchange(by_pair, p_me, lambda q: chi.at[p_me], chi, s_c, r_c)
    started += c_copies

    for c in v_copies:
        c.wait_recv()
    v_form = to_matrix(dot(pick, rows64(vt[...]).astype(BF16))).astype(BF16)
    scaled = dot(v_form, occ_cols).astype(BF16)
    energy = dot(scaled, form)
    xo[...] = dot(put, to_tiles(energy).astype(BF16)).reshape(8, 8, 1024).astype(BF16)
    x_copies = exchange(by_pair, p_me, lambda q: xo.at[q], xr, s_x, r_x)
    started += x_copies
    xr[p_me] = xo[p_me]

    for c in c_copies:
        c.wait_recv()
    chi_sum = jnp.sum(chi[...], axis=0)
    turned = pltpu.roll(chi_sum, lax.rem(128 - 5 * p_me, 128), 1)
    pol_ref[...] = turned[:, :5]

    for c in x_copies:
        c.wait_recv()
    block_sum = jnp.sum(xr[...].astype(F32), axis=0)
    for j in range(8):
        yo[j] = block_sum[:, j * 128 : (j + 1) * 128]
    y_copies = exchange(by_group, j_me, lambda j: yo.at[j], yr, s_y, r_y)
    started += y_copies
    yr[j_me] = yo[j_me]
    for c in y_copies:
        c.wait_recv()
    ar[zh_me] = jnp.sum(yr[...], axis=0)
    a_copies = exchange(by_zh, zh_me, lambda h: ar.at[zh_me], ar, s_a, r_a)
    started += a_copies
    for c in a_copies:
        c.wait_recv()
    scale = -1.0 / math.sqrt(n_aux * 8 * NAT * OA * NAT)
    fin[j_me] = jnp.sum(ar[...], axis=0) * scale
    f_copies = exchange(by_group, j_me, lambda j: fin.at[j_me], fin, s_f, r_f)
    started += f_copies
    for c in f_copies:
        c.wait_recv()
    for j in range(8):
        self_ref[:, j * 128 : (j + 1) * 128] = fin[j]
    for c in started:
        c.wait_send()


def solution(mesh):
    n_aux, n_pair = mesh.shape["aux"], mesh.shape["pair"]

    def per_device(three_center, tile_live, pair_atoms, green_occ, green_vir, screened):
        tiles = pltpu.VMEM((8, 8, 1024), BF16)
        pieces = pltpu.VMEM((8, 8, 128), F32)
        sems = pltpu.SemaphoreType.DMA((7,))
        return pl.pallas_call(
            functools.partial(kernel, n_aux, n_pair),
            out_shape=(
                jax.ShapeDtypeStruct((8, 5), F32),
                jax.ShapeDtypeStruct((8, 1024), F32),
            ),
            in_specs=[pl.BlockSpec(memory_space=pl.ANY)] * 6,
            out_specs=[pl.BlockSpec(memory_space=pltpu.VMEM)] * 2,
            scratch_shapes=[
                tiles,
                pltpu.VMEM((1, 8), jnp.int32),
                pltpu.VMEM((1, 64), jnp.int32),
                pltpu.VMEM((256, 256), BF16),
                pltpu.VMEM((256, 256), BF16),
                pltpu.VMEM((8, 40), BF16),
                pltpu.VMEM((5, 8, 8, 1024), BF16),
                *[tiles] * 7,
                *[pieces] * 5,
                pltpu.SemaphoreType.DMA((6,)),
                pltpu.SemaphoreType.DMA((4,)),
                pltpu.SemaphoreType.DMA((4,)),
                *[sems] * 16,
            ],
            compiler_params=pltpu.CompilerParams(
                collective_id=0, has_side_effects=True, vmem_limit_bytes=40 << 20
            ),
        )(three_center, tile_live, pair_atoms.reshape(1, 64), green_occ, green_vir, screened)

    placed = (P("aux", "pair", None), P("aux", "pair"), P(), P(), P(), P("aux", None))
    return jax.shard_map(
        per_device,
        mesh=mesh,
        in_specs=placed,
        out_specs=(P("aux", "pair"), P("pair", None)),
        check_vma=False,
    )
```

time: 137 us -> 57.5 us (0.42)
  starting transfers between devices: 53.9 us -> 0 us
  Pallas kernels: 0 us -> 50.5 us
  waiting for transfers between devices: 50.4 us -> 0 us
  other arithmetic: 12.3 us -> 0 us
  local copies, waits for them, and re-layouts: 15.2 us -> 5.26 us
  matrix products: 3.47 us -> 0 us
    pallas_call x0 -> x1, Pallas kernels: none -> 50.5 us  [per_device(): pl.pallas_call(functools.partial(kernel, n_aux, n_pair), out_shape=(jax.S...]
    all_to_all x6 -> x0, waiting for transfers between devices: 44.4 us -> none  [the longest x3 25.8 us: summed_on_arrival(): lax.all_to_all(in_blocks(array, dim, peers), axis, 0, 0, tiled=True)]
    all_to_all x6 -> x0, starting transfers between devices: 42 us -> none  [the longest x3 24.6 us: summed_on_arrival(): lax.all_to_all(in_blocks(array, dim, peers), axis, 0, 0, tiled=True)]
    ppermute x4 -> x0, starting transfers between devices: 11.9 us -> none  [shifted(): lax.ppermute(value, axis, [(source, source + steps) for source in range(i...]
    ppermute x4 -> x0, waiting for transfers between devices: 6.05 us -> none  [shifted(): lax.ppermute(value, axis, [(source, source + steps) for source in range(i...]
    dot_general x6 -> x0, matrix products: 3.47 us -> none  [the longest x1 1.26 us: energy_rows(): jnp.einsum('qkms,qsn->kmn', scaled_rows, orbital_form, preferred_element_...]
    gather x5 -> x0, local copies, waits for them, and re-layouts: 2.9 us -> none  [the longest x3 1.58 us: matrix_to_tiles(): return jnp.take(ordered, pair_atoms, axis=1)]
    sort x1 -> x0, other arithmetic: 2.69 us -> none  [per_device(): inverse = jnp.argsort(pair_atoms)]
  transfers between devices with their start and end apart: 10 -> 0, of which waited for: 6 -> 0; matrix products, arithmetic and copies ran while one was open for 12% -> 0% of each run, Pallas kernels for 0% -> 0%
where the time goes in v1:
time: 57.5 us; the launch traced here: 56.4 us
  Pallas kernels  50.5 us (88%)
  local copies, waits for them, and re-layouts  5.26 us (9%)
  between operations  0.66 us (1%)
    pallas_call x1, Pallas kernels, per_device(): pl.pallas_call(functools.partial(kernel, n_aux, n_pair), out_shape=(jax.S...  50.5 us
    unnamed x14, local copies, waits for them, and re-layouts  5.26 us

profile of v1, /device:TPU:1, one launch (start us, length us, event | category | flops | bytes accessed | tf_op | source)
XLA Modules:
  0.0 56.4 jit_solution(2020866728687366831)
XLA Ops:
  0.6 0.0 copy-start.5
  0.6 0.0 copy-start.4
  0.7 0.6 %copy-done.5 = s32[64]{0:T(128)S(1)} copy-done((s32[64]{0:T(128)S(1)}, s32[64]{0:T(128)}, u32[]{:S(2)}) %copy-start.5) | copy-done | bytes 280
  1.3 0.0 copy-done.4
  1.3 0.0 copy-start
  1.3 0.9 %copy-done = bf16[8,8,1024]{2,1,0:T(8,128)(2,1)S(1)} copy-done((bf16[8,8,1024]{2,1,0:T(8,128)(2,1)S(1)}, bf16[8,8,1024]{2,1,0:T(8,128)(2,1)}, u32[]{:S(2)}) %copy-start) | copy-done | bytes 131096
  2.2 0.0 copy-start.1
  2.2 0.9 %copy-done.1 = bf16[256,256]{1,0:T(8,128)(2,1)S(1)} copy-done((bf16[256,256]{1,0:T(8,128)(2,1)S(1)}, bf16[256,256]{1,0:T(8,128)(2,1)}, u32[]{:S(2)}) %copy-start.1) | copy-done | bytes 131096
  3.1 0.0 copy-start.2
  3.1 0.9 %copy-done.2 = bf16[256,256]{1,0:T(8,128)(2,1)S(1)} copy-done((bf16[256,256]{1,0:T(8,128)(2,1)S(1)}, bf16[256,256]{1,0:T(8,128)(2,1)}, u32[]{:S(2)}) %copy-start.2) | copy-done | bytes 131096
  4.0 0.0 copy-start.3
  4.0 0.7 %copy-done.3 = bf16[8,40]{1,0:T(8,128)(2,1)S(1)} copy-done((bf16[8,40]{1,0:T(8,128)(2,1)S(1)}, bf16[8,40]{1,0:T(8,128)(2,1)}, u32[]{:S(2)}) %copy-start.3) | copy-done | bytes 664
  4.7 50.5 %shard_map.77 = (f32[8,5]{1,0:T(8,128)S(1)}, f32[8,1024]{1,0:T(8,128)S(1)}) custom-call(bf16[8,8,1024]{2,1,0:T(8,128)(2,1)S(1)} %copy-done, s32[1,8]{1,0:T(1,128)S(1)} %copy-done.4, s32[1,64]{1,0:T(1,128)S(1)} %bitcast.1, bf16[256,256]{1,0:T(8,128)(2,1)S(1)} %copy-done.1, bf16[256,256]{1,0:T(8,128)(2,1)S(1)} %copy-done.2, bf16[8,40]{1,0:T(8,128)(2,1)S(1)} %copy-done.3), custom_call_target="tpu_custom_call" | custom-call | tf_op jit(solution)/shard_map/pallas_call | solution.py:321
  55.2 0.6 %copy.10 = f32[8,5]{1,0:T(8,128)} copy(f32[8,5]{1,0:T(8,128)S(1)} %get-tuple-element.4) | data formatting | bytes 320
  55.8 0.6 %copy.11 = f32[8,1024]{1,0:T(8,128)} copy(f32[8,1024]{1,0:T(8,128)S(1)} %get-tuple-element.5) | data formatting | bytes 65536
Async XLA Ops:
  0.6 0.7 %copy-start.5 = (s32[64]{0:T(128)S(1)}, s32[64]{0:T(128)}, u32[]{:S(2)}) copy-start(s32[64]{0:T(128)} %param.8) | copy-start | bytes 772
  0.6 0.7 %copy-start.4 = (s32[1,8]{1,0:T(1,128)S(1)}, s32[1,8]{1,0:T(1,128)}, u32[]{:S(2)}) copy-start(s32[1,8]{1,0:T(1,128)} %live_hbm.1) | copy-start | bytes 100
  1.3 0.9 %copy-start = (bf16[8,8,1024]{2,1,0:T(8,128)(2,1)S(1)}, bf16[8,8,1024]{2,1,0:T(8,128)(2,1)}, u32[]{:S(2)}) copy-start(bf16[8,8,1024]{2,1,0:T(8,128)(2,1)} %tc_hbm.1) | copy-start | bytes 393220
  2.2 0.9 %copy-start.1 = (bf16[256,256]{1,0:T(8,128)(2,1)S(1)}, bf16[256,256]{1,0:T(8,128)(2,1)}, u32[]{:S(2)}) copy-start(bf16[256,256]{1,0:T(8,128)(2,1)} %occ_hbm.1) | copy-start | bytes 393220
  3.1 0.9 %copy-start.2 = (bf16[256,256]{1,0:T(8,128)(2,1)S(1)}, bf16[256,256]{1,0:T(8,128)(2,1)}, u32[]{:S(2)}) copy-start(bf16[256,256]{1,0:T(8,128)(2,1)} %vir_hbm.1) | copy-start | bytes 393220
  4.0 0.7 %copy-start.3 = (bf16[8,40]{1,0:T(8,128)(2,1)S(1)}, bf16[8,40]{1,0:T(8,128)(2,1)}, u32[]{:S(2)}) copy-start(bf16[8,40]{1,0:T(8,128)(2,1)} %scr_hbm.1) | copy-start | bytes 1924

commit v2 on v1

--- a/solution.py
+++ b/solution.py
@@ -96,8 +96,6 @@
     xo,
     xr,
     chi,
-    yo,
-    yr,
     ar,
     fin,
     in_sem,
@@ -113,8 +111,6 @@
     r_x,
     s_c,
     r_c,
-    s_y,
-    r_y,
     s_a,
     r_a,
     s_f,
@@ -123,8 +119,6 @@
     a_me = lax.axis_index("aux")
     p_me = lax.axis_index("pair")
     x_me, z_me = a_me // NZ, a_me % NZ
-    zh_me, par_me = z_me // 2, z_me % 2
-    j_me = x_me * 2 + par_me
 
     loads = [
         pltpu.make_async_copy(src, dst, in_sem.at[i])
@@ -146,13 +140,18 @@
         q = lax.rem(p_me + step, n_pair)
         return q, (a_me, q)
 
-    def by_group(step):
-        j = lax.rem(j_me + step, 8)
-        return j, ((j // 2) * NZ + zh_me * 2 + lax.rem(j, 2), p_me)
-
-    def by_zh(step):
-        h = lax.rem(zh_me + step, 8)
-        return h, (x_me * NZ + h * 2 + par_me, p_me)
+    def by_plane(step):
+        q = lax.rem(p_me + step % 8, n_pair)
+        x = lax.rem(x_me + step // 8, NX)
+        return q, x, (x * NZ + z_me, q)
+
+    def by_z(step):
+        z = lax.rem(z_me + step, NZ)
+        return z, (x_me * NZ + z, p_me)
+
+    def by_x(step):
+        x = lax.rem(x_me + step, NX)
+        return x, (x * NZ + z_me, p_me)
 
     offsets = (1, -1, 2, -2)
 
@@ -160,11 +159,11 @@
         return (lax.rem(a_me + d + n_aux, n_aux), p_me)
 
     barrier = pltpu.get_barrier_semaphore()
-    for d in offsets:
-        pl.semaphore_signal(barrier, inc=1, device_id=by_window(d), device_id_type=MESH)
-    for step in range(1, 8):
-        for peer in (by_pair, by_group, by_zh):
-            pl.semaphore_signal(barrier, inc=1, device_id=peer(step)[1], device_id_type=MESH)
+    peers = [by_z(step)[-1] for step in range(1, NZ)]
+    peers += [by_plane(step)[-1] for step in range(1, 32)]
+    peers += [by_window(d) for d in offsets]
+    for device in peers:
+        pl.semaphore_signal(barrier, inc=1, device_id=device, device_id_type=MESH)
 
     def remote(src, dst, send, recv, device):
         return pltpu.make_async_remote_copy(
@@ -176,12 +175,11 @@
             device_id_type=MESH,
         )
 
-    def exchange(peer, me, source, dest, send, recv):
+    def exchange(peer, count, source, dest, send, recv):
         copies = []
-        for step in range(1, 8):
-            there, device = peer(step)
-            src = source(there)
-            copies.append(remote(src, dest.at[me], send.at[step - 1], recv.at[step - 1], device))
+        for step in range(1, count):
+            *there, device = peer(step)
+            copies.append(remote(source(*there), dest, send.at[step - 1], recv.at[step - 1], device))
         for c in copies:
             c.start()
         return copies
@@ -194,7 +192,7 @@
     )
     win[REACH] = (tc[...].astype(F32) * live_col[None]).astype(BF16)
 
-    pl.semaphore_wait(barrier, 25)
+    pl.semaphore_wait(barrier, len(peers))
     started = []
     window_copies = {}
     for i, d in enumerate(offsets):
@@ -202,7 +200,7 @@
         c.start()
         window_copies[REACH - d] = c
         started.append(c)
-    m_copies = exchange(by_pair, p_me, lambda q: win.at[REACH, q], mt, s_m, r_m)
+    m_copies = exchange(by_pair, 8, lambda q: win.at[REACH, q], mt.at[p_me], s_m, r_m)
     started += m_copies
     mt[p_me] = win[REACH, p_me]
 
@@ -239,7 +237,7 @@
     product = dot(left, vir[...])
     z_tiles = dot(put, to_tiles(product).astype(BF16))
     zo[...] = z_tiles.reshape(8, 8, 1024).astype(BF16)
-    z_copies = exchange(by_pair, p_me, lambda q: zo.at[q], zt, s_z, r_z)
+    z_copies = exchange(by_pair, 8, lambda q: zo.at[q], zt.at[p_me], s_z, r_z)
     started += z_copies
     zt[p_me] = zo[p_me]
 
@@ -248,7 +246,7 @@
         window_copies[slot].wait_recv()
         mixed += dot(couple[slot], rows64(win[slot]).astype(BF16))
     vo[...] = mixed.reshape(8, 8, 1024).astype(BF16)
-    v_copies = exchange(by_pair, p_me, lambda q: vo.at[q], vt, s_v, r_v)
+    v_copies = exchange(by_pair, 8, lambda q: vo.at[q], vt.at[p_me], s_v, r_v)
     started += v_copies
     vt[p_me] = vo[p_me]
 
@@ -265,7 +263,7 @@
         gather = jnp.where(iota((64, 128), 1) == slot * 8 + iota((64, 128), 0) // 8, 1.0, 0.0)
         chi_total += jnp.dot(terms, gather, precision=lax.Precision.HIGHEST, preferred_element_type=F32)
     chi[p_me] = chi_total * (1.0 / (OA * NAT))
-    c_copies = exchange(by_pair, p_me, lambda q: chi.at[p_me], chi, s_c, r_c)
+    c_copies = exchange(by_pair, 8, lambda q: chi.at[p_me], chi.at[p_me], s_c, r_c)
     started += c_copies
 
     for c in v_copies:
@@ -273,10 +271,11 @@
     v_form = to_matrix(dot(pick, rows64(vt[...]).astype(BF16))).astype(BF16)
     scaled = dot(v_form, occ_cols).astype(BF16)
     energy = dot(scaled, form)
-    xo[...] = dot(put, to_tiles(energy).astype(BF16)).reshape(8, 8, 1024).astype(BF16)
-    x_copies = exchange(by_pair, p_me, lambda q: xo.at[q], xr, s_x, r_x)
-    started += x_copies
-    xr[p_me] = xo[p_me]
+    energy_tiles = dot(put, to_tiles(energy).astype(BF16))
+    for x in range(NX):
+        xo[:, x] = energy_tiles[:, x * 256 : (x + 1) * 256].reshape(8, 8, 256).astype(BF16)
+    x_copies = exchange(by_plane, 32, lambda q, x: xo.at[q, x], xr.at[x_me * 8 + p_me], s_x, r_x)
+    xr[x_me * 8 + p_me] = xo[p_me, x_me]
 
     for c in c_copies:
         c.wait_recv()
@@ -286,28 +285,22 @@
 
     for c in x_copies:
         c.wait_recv()
-    block_sum = jnp.sum(xr[...].astype(F32), axis=0)
-    for j in range(8):
-        yo[j] = block_sum[:, j * 128 : (j + 1) * 128]
-    y_copies = exchange(by_group, j_me, lambda j: yo.at[j], yr, s_y, r_y)
-    started += y_copies
-    yr[j_me] = yo[j_me]
-    for c in y_copies:
-        c.wait_recv()
-    ar[zh_me] = jnp.sum(yr[...], axis=0)
-    a_copies = exchange(by_zh, zh_me, lambda h: ar.at[zh_me], ar, s_a, r_a)
-    started += a_copies
+    ar[z_me] = jnp.sum(xr[...].astype(F32), axis=0).astype(BF16)
+    a_copies = exchange(by_z, NZ, lambda z: ar.at[z_me], ar.at[z_me], s_a, r_a)
+    for c in started + x_copies:
+        c.wait_send()
     for c in a_copies:
         c.wait_recv()
     scale = -1.0 / math.sqrt(n_aux * 8 * NAT * OA * NAT)
-    fin[j_me] = jnp.sum(ar[...], axis=0) * scale
-    f_copies = exchange(by_group, j_me, lambda j: fin.at[j_me], fin, s_f, r_f)
-    started += f_copies
+    fin[x_me] = jnp.sum(ar[...].astype(F32), axis=0) * scale
+    f_copies = exchange(by_x, NX, lambda x: fin.at[x_me], fin.at[x_me], s_f, r_f)
+    for c in a_copies:
+        c.wait_send()
     for c in f_copies:
         c.wait_recv()
-    for j in range(8):
-        self_ref[:, j * 128 : (j + 1) * 128] = fin[j]
-    for c in started:
+    for x in range(NX):
+        self_ref[:, x * 256 : (x + 1) * 256] = fin[x]
+    for c in f_copies:
         c.wait_send()
 
 
@@ -316,7 +309,6 @@
 
     def per_device(three_center, tile_live, pair_atoms, green_occ, green_vir, screened):
         tiles = pltpu.VMEM((8, 8, 1024), BF16)
-        pieces = pltpu.VMEM((8, 8, 128), F32)
         sems = pltpu.SemaphoreType.DMA((7,))
         return pl.pallas_call(
             functools.partial(kernel, n_aux, n_pair),
@@ -334,17 +326,37 @@
                 pltpu.VMEM((256, 256), BF16),
                 pltpu.VMEM((8, 40), BF16),
                 pltpu.VMEM((5, 8, 8, 1024), BF16),
-                *[tiles] * 7,
-                *[pieces] * 5,
+                *[tiles] * 5,
+                pltpu.VMEM((8, NX, 8, 256), BF16),
+                pltpu.VMEM((32, 8, 256), BF16),
+                pltpu.VMEM((8, 8, 128), F32),
+                pltpu.VMEM((NZ, 8, 256), BF16),
+                pltpu.VMEM((NX, 8, 256), F32),
                 pltpu.SemaphoreType.DMA((6,)),
                 pltpu.SemaphoreType.DMA((4,)),
                 pltpu.SemaphoreType.DMA((4,)),
-                *[sems] * 16,
+                *[sems] * 6,
+                *[pltpu.SemaphoreType.DMA((31,))] * 2,
+                *[sems] * 2,
+                *[pltpu.SemaphoreType.DMA((15,))] * 2,
+                *[sems] * 2,
             ],
             compiler_params=pltpu.CompilerParams(
                 collective_id=0, has_side_effects=True, vmem_limit_bytes=40 << 20
             ),
-        )(three_center, tile_live, pair_atoms.reshape(1, 64), green_occ, green_vir, screened)
+        )(
+            *(
+                pltpu.with_memory_space_constraint(v, pltpu.HBM)
+                for v in (
+                    three_center,
+                    tile_live,
+                    pair_atoms.reshape(1, 64),
+                    green_occ,
+                    green_vir,
+                    screened,
+                )
+            )
+        )
 
     placed = (P("aux", "pair", None), P("aux", "pair"), P(), P(), P(), P("aux", None))
     return jax.shard_map(

time: 57.5 us -> 50.6 us (0.88); the launches traced: 56.4 us -> 50.5 us
  local copies, waits for them, and re-layouts: 5.26 us -> 1.21 us
  Pallas kernels: 50.5 us -> 48.6 us
    unnamed x14 -> x2, local copies, waits for them, and re-layouts: 5.26 us -> 1.21 us
    pallas_call x1, Pallas kernels: 50.5 us -> 48.6 us  [per_device(): pl.pallas_call(functools.partial(kernel, n_aux, n_pair), out_shape=(jax.S...]
where the time goes in v2:
time: 50.6 us; the launch traced here: 50.5 us
  Pallas kernels  48.6 us (96%)
  local copies, waits for them, and re-layouts  1.21 us (2%)
  between operations  0.64 us (1%)
    pallas_call x1, Pallas kernels, per_device(): pl.pallas_call(functools.partial(kernel, n_aux, n_pair), out_shape=(jax.S...  48.6 us
    unnamed x2, local copies, waits for them, and re-layouts  1.21 us

profile of v2, /device:TPU:1, one launch (start us, length us, event | category | flops | bytes accessed | tf_op | source)
XLA Modules:
  0.0 50.5 jit_solution(9180270186136845659)
XLA Ops:
  0.6 48.6 %shard_map.77 = (f32[8,5]{1,0:T(8,128)S(1)}, f32[8,1024]{1,0:T(8,128)S(1)}) custom-call(bf16[8,8,1024]{2,1,0:T(8,128)(2,1)} %tc_hbm.1, s32[1,8]{1,0:T(1,128)} %live_hbm.1, s32[1,64]{1,0:T(1,128)} %bitcast.1, bf16[256,256]{1,0:T(8,128)(2,1)} %occ_hbm.1, bf16[256,256]{1,0:T(8,128)(2,1)} %vir_hbm.1, bf16[8,40]{1,0:T(8,128)(2,1)} %scr_hbm.1), custom_call_target="tpu_custom_call" | custom-call | tf_op jit(solution)/shard_map/pallas_call | solution.py:313
  49.3 0.6 %copy.10 = f32[8,5]{1,0:T(8,128)} copy(f32[8,5]{1,0:T(8,128)S(1)} %get-tuple-element.4) | data formatting | bytes 320
  49.9 0.6 %copy.11 = f32[8,1024]{1,0:T(8,128)} copy(f32[8,1024]{1,0:T(8,128)S(1)} %get-tuple-element.5) | data formatting | bytes 65536

commit v3 on v2

--- a/solution.py
+++ b/solution.py
@@ -115,6 +115,7 @@
     r_a,
     s_f,
     r_f,
+    known,
 ):
     a_me = lax.axis_index("aux")
     p_me = lax.axis_index("pair")
@@ -159,9 +160,11 @@
         return (lax.rem(a_me + d + n_aux, n_aux), p_me)
 
     barrier = pltpu.get_barrier_semaphore()
-    peers = [by_z(step)[-1] for step in range(1, NZ)]
-    peers += [by_plane(step)[-1] for step in range(1, 32)]
-    peers += [by_window(d) for d in offsets]
+    near = (1, NZ - 1, 2, NZ - 2)
+    peers = [by_window(d) for d in offsets]
+    peers += [by_x(step)[-1] for step in (2, 1, 3)]
+    peers += [by_pair(step)[-1] for step in range(1, 8)]
+    peers += [by_z(step)[-1] for step in near]
     for device in peers:
         pl.semaphore_signal(barrier, inc=1, device_id=device, device_id_type=MESH)
 
@@ -193,6 +196,8 @@
     win[REACH] = (tc[...].astype(F32) * live_col[None]).astype(BF16)
 
     pl.semaphore_wait(barrier, len(peers))
+    for step in (2, NZ - 2):
+        pl.semaphore_signal(known.at[0], inc=1, device_id=by_z(step)[-1], device_id_type=MESH)
     started = []
     window_copies = {}
     for i, d in enumerate(offsets):
@@ -241,6 +246,10 @@
     started += z_copies
     zt[p_me] = zo[p_me]
 
+    pl.semaphore_wait(known.at[0], 2)
+    for step in (4, NZ - 4):
+        pl.semaphore_signal(known.at[1], inc=1, device_id=by_z(step)[-1], device_id_type=MESH)
+
     mixed = dot(couple[2], rows64(win[2]).astype(BF16))
     for slot in (1, 3, 0, 4):
         window_copies[slot].wait_recv()
@@ -286,6 +295,7 @@
     for c in x_copies:
         c.wait_recv()
     ar[z_me] = jnp.sum(xr[...].astype(F32), axis=0).astype(BF16)
+    pl.semaphore_wait(known.at[1], 2)
     a_copies = exchange(by_z, NZ, lambda z: ar.at[z_me], ar.at[z_me], s_a, r_a)
     for c in started + x_copies:
         c.wait_send()
@@ -340,6 +350,7 @@
                 *[sems] * 2,
                 *[pltpu.SemaphoreType.DMA((15,))] * 2,
                 *[sems] * 2,
+                pltpu.SemaphoreType.REGULAR((2,)),
             ],
             compiler_params=pltpu.CompilerParams(
                 collective_id=0, has_side_effects=True, vmem_limit_bytes=40 << 20

time: 50.6 us -> 48.3 us (0.955)
  Pallas kernels: 48.6 us -> 46 us
    pallas_call x1, Pallas kernels: 48.6 us -> 46 us  [per_device(): pl.pallas_call(functools.partial(kernel, n_aux, n_pair), out_shape=(jax.S...]
where the time goes in v3:
time: 48.3 us; the launch traced here: 47.8 us
  Pallas kernels  46 us (95%)
  local copies, waits for them, and re-layouts  1.21 us (3%)
  between operations  0.64 us (1%)
    pallas_call x1, Pallas kernels, per_device(): pl.pallas_call(functools.partial(kernel, n_aux, n_pair), out_shape=(jax.S...  46 us
    unnamed x2, local copies, waits for them, and re-layouts  1.21 us

profile of v3, /device:TPU:1, one launch (start us, length us, event | category | flops | bytes accessed | tf_op | source)
XLA Modules:
  0.0 47.8 jit_solution(2164388456564831566)
XLA Ops:
  0.6 46.0 %shard_map.77 = (f32[8,5]{1,0:T(8,128)S(1)}, f32[8,1024]{1,0:T(8,128)S(1)}) custom-call(bf16[8,8,1024]{2,1,0:T(8,128)(2,1)} %tc_hbm.1, s32[1,8]{1,0:T(1,128)} %live_hbm.1, s32[1,64]{1,0:T(1,128)} %bitcast.1, bf16[256,256]{1,0:T(8,128)(2,1)} %occ_hbm.1, bf16[256,256]{1,0:T(8,128)(2,1)} %vir_hbm.1, bf16[8,40]{1,0:T(8,128)(2,1)} %scr_hbm.1), custom_call_target="tpu_custom_call" | custom-call | tf_op jit(solution)/shard_map/pallas_call | solution.py:323
  46.6 0.6 %copy.10 = f32[8,5]{1,0:T(8,128)} copy(f32[8,5]{1,0:T(8,128)S(1)} %get-tuple-element.4) | data formatting | bytes 320
  47.2 0.6 %copy.11 = f32[8,1024]{1,0:T(8,128)} copy(f32[8,1024]{1,0:T(8,128)S(1)} %get-tuple-element.5) | data formatting | bytes 65536

commit v4 on v2

--- a/solution.py
+++ b/solution.py
@@ -101,6 +101,8 @@
     in_sem,
     s_win,
     r_win,
+    s_far,
+    r_far,
     s_m,
     r_m,
     s_z,
@@ -115,6 +117,7 @@
     r_a,
     s_f,
     r_f,
+    known,
 ):
     a_me = lax.axis_index("aux")
     p_me = lax.axis_index("pair")
@@ -153,17 +156,26 @@
         x = lax.rem(x_me + step, NX)
         return x, (x * NZ + z_me, p_me)
 
-    offsets = (1, -1, 2, -2)
+    offsets = (1, -1)
+    chunks = [pl.ds(2 * c, 2) for c in range(4)]
 
     def by_window(d):
         return (lax.rem(a_me + d + n_aux, n_aux), p_me)
 
     barrier = pltpu.get_barrier_semaphore()
-    peers = [by_z(step)[-1] for step in range(1, NZ)]
-    peers += [by_plane(step)[-1] for step in range(1, 32)]
-    peers += [by_window(d) for d in offsets]
+    peers = [by_window(d) for d in offsets]
+    peers += [by_x(step)[-1] for step in (2, 1, 3)]
+    peers += [by_pair(step)[-1] for step in range(1, 8)]
+    peers += [by_z(step)[-1] for step in (1, NZ - 1)]
     for device in peers:
         pl.semaphore_signal(barrier, inc=1, device_id=device, device_id_type=MESH)
+
+    def tell(r):
+        for step in (1 << r, NZ - (1 << r)):
+            pl.semaphore_signal(known.at[r], inc=1, device_id=by_z(step)[-1], device_id_type=MESH)
+
+    def hear(r):
+        pl.semaphore_wait(known.at[r], 2)
 
     def remote(src, dst, send, recv, device):
         return pltpu.make_async_remote_copy(
@@ -194,12 +206,14 @@
 
     pl.semaphore_wait(barrier, len(peers))
     started = []
-    window_copies = {}
-    for i, d in enumerate(offsets):
-        c = remote(win.at[REACH], win.at[REACH - d], s_win.at[i], r_win.at[i], by_window(d))
-        c.start()
-        window_copies[REACH - d] = c
-        started.append(c)
+    arriving = {1: [], 3: []}
+    for c, part in enumerate(chunks):
+        for i, d in enumerate(offsets):
+            copy = remote(
+                win.at[REACH, part], win.at[REACH - d, part], s_win.at[i, c], r_win.at[i, c], by_window(d)
+            )
+            copy.start()
+            arriving[REACH - d].append(copy)
     m_copies = exchange(by_pair, 8, lambda q: win.at[REACH, q], mt.at[p_me], s_m, r_m)
     started += m_copies
     mt[p_me] = win[REACH, p_me]
@@ -230,6 +244,22 @@
         keep = jnp.logical_and(same_tile, inside)
         couple.append(jnp.where(keep, dot(wide, spread.astype(BF16)), 0.0).astype(BF16))
 
+    tell(0)
+    relayed = {0: [], 4: []}
+    for c, part in enumerate(chunks):
+        for i, d in enumerate(offsets):
+            arriving[REACH - d][c].wait_recv()
+            copy = remote(
+                win.at[REACH - d, part],
+                win.at[REACH - 2 * d, part],
+                s_far.at[i, c],
+                r_far.at[i, c],
+                by_window(d),
+            )
+            copy.start()
+            relayed[REACH - 2 * d].append(copy)
+    started += arriving[1] + arriving[3] + relayed[0] + relayed[4]
+
     for c in m_copies:
         c.wait_recv()
     form = to_matrix(dot(pick, rows64(mt[...]).astype(BF16))).astype(BF16)
@@ -241,15 +271,20 @@
     started += z_copies
     zt[p_me] = zo[p_me]
 
+    hear(0)
+    tell(1)
     mixed = dot(couple[2], rows64(win[2]).astype(BF16))
     for slot in (1, 3, 0, 4):
-        window_copies[slot].wait_recv()
+        for c in relayed.get(slot, ()):
+            c.wait_recv()
         mixed += dot(couple[slot], rows64(win[slot]).astype(BF16))
     vo[...] = mixed.reshape(8, 8, 1024).astype(BF16)
     v_copies = exchange(by_pair, 8, lambda q: vo.at[q], vt.at[p_me], s_v, r_v)
     started += v_copies
     vt[p_me] = vo[p_me]
 
+    hear(1)
+    tell(2)
     for c in z_copies:
         c.wait_recv()
     z_rows = rows64(zt[...]).astype(BF16)
@@ -286,6 +321,7 @@
     for c in x_copies:
         c.wait_recv()
     ar[z_me] = jnp.sum(xr[...].astype(F32), axis=0).astype(BF16)
+    hear(2)
     a_copies = exchange(by_z, NZ, lambda z: ar.at[z_me], ar.at[z_me], s_a, r_a)
     for c in started + x_copies:
         c.wait_send()
@@ -333,13 +369,13 @@
                 pltpu.VMEM((NZ, 8, 256), BF16),
                 pltpu.VMEM((NX, 8, 256), F32),
                 pltpu.SemaphoreType.DMA((6,)),
-                pltpu.SemaphoreType.DMA((4,)),
-                pltpu.SemaphoreType.DMA((4,)),
+                *[pltpu.SemaphoreType.DMA((2, 4))] * 4,
                 *[sems] * 6,
                 *[pltpu.SemaphoreType.DMA((31,))] * 2,
                 *[sems] * 2,
                 *[pltpu.SemaphoreType.DMA((15,))] * 2,
                 *[sems] * 2,
+                pltpu.SemaphoreType.REGULAR((3,)),
             ],
             compiler_params=pltpu.CompilerParams(
                 collective_id=0, has_side_effects=True, vmem_limit_bytes=40 << 20

time: 50.6 us -> 47.1 us (0.931)
  Pallas kernels: 48.6 us -> 44.8 us
    pallas_call x1, Pallas kernels: 48.6 us -> 44.8 us  [per_device(): pl.pallas_call(functools.partial(kernel, n_aux, n_pair), out_shape=(jax.S...]
where the time goes in v4:
time: 47.1 us; the launch traced here: 46.6 us
  Pallas kernels  44.8 us (95%)
  local copies, waits for them, and re-layouts  1.21 us (3%)
  between operations  0.64 us (1%)
    pallas_call x1, Pallas kernels, per_device(): pl.pallas_call(functools.partial(kernel, n_aux, n_pair), out_shape=(jax.S...  44.8 us
    unnamed x2, local copies, waits for them, and re-layouts  1.21 us

profile of v4, /device:TPU:1, one launch (start us, length us, event | category | flops | bytes accessed | tf_op | source)
XLA Modules:
  0.0 46.6 jit_solution(17270353166819131175)
XLA Ops:
  0.6 44.8 %shard_map.77 = (f32[8,5]{1,0:T(8,128)S(1)}, f32[8,1024]{1,0:T(8,128)S(1)}) custom-call(bf16[8,8,1024]{2,1,0:T(8,128)(2,1)} %tc_hbm.1, s32[1,8]{1,0:T(1,128)} %live_hbm.1, s32[1,64]{1,0:T(1,128)} %bitcast.1, bf16[256,256]{1,0:T(8,128)(2,1)} %occ_hbm.1, bf16[256,256]{1,0:T(8,128)(2,1)} %vir_hbm.1, bf16[8,40]{1,0:T(8,128)(2,1)} %scr_hbm.1), custom_call_target="tpu_custom_call" | custom-call | tf_op jit(solution)/shard_map/pallas_call | solution.py:349
  45.4 0.6 %copy.10 = f32[8,5]{1,0:T(8,128)} copy(f32[8,5]{1,0:T(8,128)S(1)} %get-tuple-element.4) | data formatting | bytes 320
  46.0 0.6 %copy.11 = f32[8,1024]{1,0:T(8,128)} copy(f32[8,1024]{1,0:T(8,128)S(1)} %get-tuple-element.5) | data formatting | bytes 65536

commit v5 on v4

--- a/solution.py
+++ b/solution.py
@@ -93,6 +93,9 @@
     zt,
     vo,
     vt,
+    held,
+    forms,
+    near,
     xo,
     xr,
     chi,
@@ -122,6 +125,8 @@
     a_me = lax.axis_index("aux")
     p_me = lax.axis_index("pair")
     x_me, z_me = a_me // NZ, a_me % NZ
+    y_me, c_me = p_me // 2, p_me % 2
+    f_me = c_me * 4 + y_me
 
     loads = [
         pltpu.make_async_copy(src, dst, in_sem.at[i])
@@ -214,9 +219,11 @@
             )
             copy.start()
             arriving[REACH - d].append(copy)
-    m_copies = exchange(by_pair, 8, lambda q: win.at[REACH, q], mt.at[p_me], s_m, r_m)
+    m_copies = exchange(
+        by_pair, 8, lambda q: win.at[REACH, pl.ds(4 * (q % 2), 4)], mt.at[p_me], s_m, r_m
+    )
     started += m_copies
-    mt[p_me] = win[REACH, p_me]
+    mt[p_me] = win[REACH, pl.ds(4 * c_me, 4)]
 
     for c in loads[2:]:
         c.wait()
@@ -234,6 +241,29 @@
     ).astype(jnp.int32)
     spot = iota((64, 64), 1)
     put = jnp.where((spot % 8) * 8 + spot // 8 == atom_col, 1.0, 0.0).astype(BF16)
+    held[...] = jnp.broadcast_to(atom_col, (64, 128))
+    own_atoms = [
+        held[pl.ds(pl.multiple_of((2 * y_me + core) * 8, 8), 8), :] for core in range(2)
+    ]
+    second = [
+        jnp.broadcast_to((v & 7)[None], (OA, 8, 128)).reshape(256, 128) for v in own_atoms
+    ]
+    wide_col = iota((8, 256), 1)
+    firsts = [
+        jnp.sum(
+            jnp.where(
+                iota((8, 256), 0) == wide_col % 8, jnp.concatenate([v, v], axis=1) >> 3, 0
+            ).astype(F32),
+            axis=0,
+            keepdims=True,
+        )
+        for v in own_atoms
+    ]
+    column = iota((64, 256), 1)
+    first = jnp.where((column // 64) % 2 == 0, firsts[0], firsts[1]).astype(jnp.int32)
+    collect = jnp.where(
+        jnp.logical_and((atom_col & 7) == (column % 64) // 8, (atom_col >> 3) == first), 1.0, 0.0
+    ).astype(BF16)
     wide = jnp.broadcast_to(scr[...].astype(F32)[:, None, :], (8, 8, 40)).reshape(64, 40).astype(BF16)
     same_tile = (iota((64, 64), 0) % 8) == (iota((64, 64), 1) % 8)
     couple = []
@@ -260,31 +290,64 @@
             relayed[REACH - 2 * d].append(copy)
     started += arriving[1] + arriving[3] + relayed[0] + relayed[4]
 
-    for c in m_copies:
-        c.wait_recv()
-    form = to_matrix(dot(pick, rows64(mt[...]).astype(BF16))).astype(BF16)
-    left = dot(occ_both, form, ((0,), (0,))).astype(BF16)
-    product = dot(left, vir[...])
-    z_tiles = dot(put, to_tiles(product).astype(BF16))
-    zo[...] = z_tiles.reshape(8, 8, 1024).astype(BF16)
-    z_copies = exchange(by_pair, 8, lambda q: zo.at[q], zt.at[p_me], s_z, r_z)
-    started += z_copies
-    zt[p_me] = zo[p_me]
-
     hear(0)
     tell(1)
+
     mixed = dot(couple[2], rows64(win[2]).astype(BF16))
     for slot in (1, 3, 0, 4):
         for c in relayed.get(slot, ()):
             c.wait_recv()
         mixed += dot(couple[slot], rows64(win[slot]).astype(BF16))
     vo[...] = mixed.reshape(8, 8, 1024).astype(BF16)
-    v_copies = exchange(by_pair, 8, lambda q: vo.at[q], vt.at[p_me], s_v, r_v)
-    started += v_copies
-    vt[p_me] = vo[p_me]
+    v_copy = remote(
+        vo.at[pl.ds(4 * (1 - c_me), 4)], vt.at[c_me], s_v, r_v, (a_me, y_me * 2 + 1 - c_me)
+    )
+    v_copy.start()
+    started.append(v_copy)
+    vt[c_me] = vo[pl.ds(4 * c_me, 4)]
+
+    for c in m_copies:
+        c.wait_recv()
+    for i in range(4):
+        form = to_matrix(dot(pick, rows64(mt[:, i]).astype(BF16))).astype(BF16)
+        forms[i] = form
+        near[:, i] = dot(occ_cols, form).reshape(NAT, OA, 256).astype(BF16)
+
+    v_copy.wait_recv()
+    v_form = to_matrix(rows64(vt[...]))
+    stacked = []
+    for core in range(2):
+        half = v_form[:, core * 128 : (core + 1) * 128]
+        stacked.append(
+            jnp.concatenate(
+                [jnp.where(second[core] == b, half, 0.0).astype(BF16) for b in range(NAT)], axis=1
+            )
+        )
+    energy = dot(jnp.concatenate(stacked, axis=0), near[...].reshape(1024, 256))
+    blocks = [to_tiles(energy[core * 256 : (core + 1) * 256]) for core in range(2)]
+    upper = [v.astype(BF16) for v in blocks]
+    lower = [(v - u.astype(F32)).astype(BF16) for v, u in zip(blocks, upper)]
+    energy_tiles = dot(collect, jnp.concatenate(upper + lower, axis=0))
+    for x in range(NX):
+        xo[:, x] = energy_tiles[:, x * 256 : (x + 1) * 256].reshape(8, 8, 256).astype(BF16)
+    x_copies = exchange(by_plane, 32, lambda q, x: xo.at[q, x], xr.at[x_me * 8 + p_me], s_x, r_x)
+    xr[x_me * 8 + p_me] = xo[p_me, x_me]
 
     hear(1)
     tell(2)
+    left = dot(occ_both, forms[y_me], ((0,), (0,))).astype(BF16)
+    z_tiles = dot(put, to_tiles(dot(left, vir[...])).astype(BF16))
+    zo[...] = z_tiles.reshape(8, 8, 1024).astype(BF16)
+    z_copies = exchange(by_pair, 8, lambda q: zo.at[q], zt.at[f_me], s_z, r_z)
+    started += z_copies
+    zt[f_me] = zo[p_me]
+
+    for c in x_copies:
+        c.wait_recv()
+    ar[z_me] = jnp.sum(xr[...].astype(F32), axis=0).astype(BF16)
+    hear(2)
+    a_copies = exchange(by_z, NZ, lambda z: ar.at[z_me], ar.at[z_me], s_a, r_a)
+
     for c in z_copies:
         c.wait_recv()
     z_rows = rows64(zt[...]).astype(BF16)
@@ -301,28 +364,6 @@
     c_copies = exchange(by_pair, 8, lambda q: chi.at[p_me], chi.at[p_me], s_c, r_c)
     started += c_copies
 
-    for c in v_copies:
-        c.wait_recv()
-    v_form = to_matrix(dot(pick, rows64(vt[...]).astype(BF16))).astype(BF16)
-    scaled = dot(v_form, occ_cols).astype(BF16)
-    energy = dot(scaled, form)
-    energy_tiles = dot(put, to_tiles(energy).astype(BF16))
-    for x in range(NX):
-        xo[:, x] = energy_tiles[:, x * 256 : (x + 1) * 256].reshape(8, 8, 256).astype(BF16)
-    x_copies = exchange(by_plane, 32, lambda q, x: xo.at[q, x], xr.at[x_me * 8 + p_me], s_x, r_x)
-    xr[x_me * 8 + p_me] = xo[p_me, x_me]
-
-    for c in c_copies:
-        c.wait_recv()
-    chi_sum = jnp.sum(chi[...], axis=0)
-    turned = pltpu.roll(chi_sum, lax.rem(128 - 5 * p_me, 128), 1)
-    pol_ref[...] = turned[:, :5]
-
-    for c in x_copies:
-        c.wait_recv()
-    ar[z_me] = jnp.sum(xr[...].astype(F32), axis=0).astype(BF16)
-    hear(2)
-    a_copies = exchange(by_z, NZ, lambda z: ar.at[z_me], ar.at[z_me], s_a, r_a)
     for c in started + x_copies:
         c.wait_send()
     for c in a_copies:
@@ -330,6 +371,11 @@
     scale = -1.0 / math.sqrt(n_aux * 8 * NAT * OA * NAT)
     fin[x_me] = jnp.sum(ar[...].astype(F32), axis=0) * scale
     f_copies = exchange(by_x, NX, lambda x: fin.at[x_me], fin.at[x_me], s_f, r_f)
+
+    for c in c_copies:
+        c.wait_recv()
+    turned = pltpu.roll(jnp.sum(chi[...], axis=0), lax.rem(128 - 5 * p_me, 128), 1)
+    pol_ref[...] = turned[:, :5]
     for c in a_copies:
         c.wait_send()
     for c in f_copies:
@@ -362,7 +408,12 @@
                 pltpu.VMEM((256, 256), BF16),
                 pltpu.VMEM((8, 40), BF16),
                 pltpu.VMEM((5, 8, 8, 1024), BF16),
-                *[tiles] * 5,
+                pltpu.VMEM((8, 4, 8, 1024), BF16),
+                *[tiles] * 3,
+                pltpu.VMEM((2, 4, 8, 1024), BF16),
+                pltpu.VMEM((64, 128), jnp.int32),
+                pltpu.VMEM((4, 256, 256), BF16),
+                pltpu.VMEM((NAT, 4, OA, 256), BF16),
                 pltpu.VMEM((8, NX, 8, 256), BF16),
                 pltpu.VMEM((32, 8, 256), BF16),
                 pltpu.VMEM((8, 8, 128), F32),
@@ -370,7 +421,8 @@
                 pltpu.VMEM((NX, 8, 256), F32),
                 pltpu.SemaphoreType.DMA((6,)),
                 *[pltpu.SemaphoreType.DMA((2, 4))] * 4,
-                *[sems] * 6,
+                *[sems] * 4,
+                *[pltpu.SemaphoreType.DMA(())] * 2,
                 *[pltpu.SemaphoreType.DMA((31,))] * 2,
                 *[sems] * 2,
                 *[pltpu.SemaphoreType.DMA((15,))] * 2,

time: 47.1 us -> 44.5 us (0.945)
  Pallas kernels: 44.8 us -> 42.5 us
    pallas_call x1, Pallas kernels: 44.8 us -> 42.5 us  [per_device(): pl.pallas_call(functools.partial(kernel, n_aux, n_pair), out_shape=(jax.S...]
where the time goes in v5:
time: 44.5 us; the launch traced here: 44.4 us
  Pallas kernels  42.5 us (96%)
  local copies, waits for them, and re-layouts  1.21 us (3%)
  between operations  0.64 us (1%)
    pallas_call x1, Pallas kernels, per_device(): pl.pallas_call(functools.partial(kernel, n_aux, n_pair), out_shape=(jax.S...  42.5 us
    unnamed x2, local copies, waits for them, and re-layouts  1.21 us

profile of v5, /device:TPU:1, one launch (start us, length us, event | category | flops | bytes accessed | tf_op | source)
XLA Modules:
  0.0 44.4 jit_solution(5297416121937098274)
XLA Ops:
  0.6 42.5 %shard_map.77 = (f32[8,5]{1,0:T(8,128)S(1)}, f32[8,1024]{1,0:T(8,128)S(1)}) custom-call(bf16[8,8,1024]{2,1,0:T(8,128)(2,1)} %tc_hbm.1, s32[1,8]{1,0:T(1,128)} %live_hbm.1, s32[1,64]{1,0:T(1,128)} %bitcast.1, bf16[256,256]{1,0:T(8,128)(2,1)} %occ_hbm.1, bf16[256,256]{1,0:T(8,128)(2,1)} %vir_hbm.1, bf16[8,40]{1,0:T(8,128)(2,1)} %scr_hbm.1), custom_call_target="tpu_custom_call" | custom-call | tf_op jit(solution)/shard_map/pallas_call | solution.py:395
  43.2 0.6 %copy.10 = f32[8,5]{1,0:T(8,128)} copy(f32[8,5]{1,0:T(8,128)S(1)} %get-tuple-element.4) | data formatting | bytes 320
  43.8 0.6 %copy.11 = f32[8,1024]{1,0:T(8,128)} copy(f32[8,1024]{1,0:T(8,128)S(1)} %get-tuple-element.5) | data formatting | bytes 65536

commit v6 on v5

--- a/solution.py
+++ b/solution.py
@@ -104,7 +104,6 @@
     in_sem,
     s_win,
     r_win,
-    s_far,
     r_far,
     s_m,
     r_m,
@@ -193,13 +192,17 @@
         )
 
     def exchange(peer, count, source, dest, send, recv):
-        copies = []
-        for step in range(1, count):
+        for step in sorted(range(1, count), key=lambda v: distance(peer, v)):
             *there, device = peer(step)
-            copies.append(remote(source(*there), dest, send.at[step - 1], recv.at[step - 1], device))
-        for c in copies:
-            c.start()
-        return copies
+            remote(source(*there), dest, send, recv, device).start()
+
+    def distance(peer, step):
+        if peer is by_plane:
+            return abs(step % 8 - 4) + 2 * abs(step // 8 - 2)
+        return abs(step - {by_pair: 4, by_z: NZ // 2, by_x: 2}[peer])
+
+    def await_all(slots, sem):
+        pltpu.make_async_copy(slots, slots, sem).wait()
 
     loads[0].wait()
     loads[1].wait()
@@ -210,19 +213,17 @@
     win[REACH] = (tc[...].astype(F32) * live_col[None]).astype(BF16)
 
     pl.semaphore_wait(barrier, len(peers))
-    started = []
     arriving = {1: [], 3: []}
     for c, part in enumerate(chunks):
         for i, d in enumerate(offsets):
             copy = remote(
-                win.at[REACH, part], win.at[REACH - d, part], s_win.at[i, c], r_win.at[i, c], by_window(d)
+                win.at[REACH, part], win.at[REACH - d, part], s_win, r_win.at[i, c], by_window(d)
             )
             copy.start()
             arriving[REACH - d].append(copy)
-    m_copies = exchange(
+    exchange(
         by_pair, 8, lambda q: win.at[REACH, pl.ds(4 * (q % 2), 4)], mt.at[p_me], s_m, r_m
     )
-    started += m_copies
     mt[p_me] = win[REACH, pl.ds(4 * c_me, 4)]
 
     for c in loads[2:]:
@@ -275,39 +276,33 @@
         couple.append(jnp.where(keep, dot(wide, spread.astype(BF16)), 0.0).astype(BF16))
 
     tell(0)
-    relayed = {0: [], 4: []}
     for c, part in enumerate(chunks):
         for i, d in enumerate(offsets):
             arriving[REACH - d][c].wait_recv()
             copy = remote(
                 win.at[REACH - d, part],
                 win.at[REACH - 2 * d, part],
-                s_far.at[i, c],
-                r_far.at[i, c],
+                s_win,
+                r_far.at[i],
                 by_window(d),
             )
             copy.start()
-            relayed[REACH - 2 * d].append(copy)
-    started += arriving[1] + arriving[3] + relayed[0] + relayed[4]
-
     hear(0)
     tell(1)
 
     mixed = dot(couple[2], rows64(win[2]).astype(BF16))
     for slot in (1, 3, 0, 4):
-        for c in relayed.get(slot, ()):
-            c.wait_recv()
+        if slot in (0, 4):
+            await_all(win.at[slot], r_far.at[slot // 4])
         mixed += dot(couple[slot], rows64(win[slot]).astype(BF16))
     vo[...] = mixed.reshape(8, 8, 1024).astype(BF16)
     v_copy = remote(
         vo.at[pl.ds(4 * (1 - c_me), 4)], vt.at[c_me], s_v, r_v, (a_me, y_me * 2 + 1 - c_me)
     )
     v_copy.start()
-    started.append(v_copy)
     vt[c_me] = vo[pl.ds(4 * c_me, 4)]
 
-    for c in m_copies:
-        c.wait_recv()
+    await_all(mt.at[pl.ds(0, 7)], r_m)
     for i in range(4):
         form = to_matrix(dot(pick, rows64(mt[:, i]).astype(BF16))).astype(BF16)
         forms[i] = form
@@ -330,7 +325,7 @@
     energy_tiles = dot(collect, jnp.concatenate(upper + lower, axis=0))
     for x in range(NX):
         xo[:, x] = energy_tiles[:, x * 256 : (x + 1) * 256].reshape(8, 8, 256).astype(BF16)
-    x_copies = exchange(by_plane, 32, lambda q, x: xo.at[q, x], xr.at[x_me * 8 + p_me], s_x, r_x)
+    exchange(by_plane, 32, lambda q, x: xo.at[q, x], xr.at[x_me * 8 + p_me], s_x, r_x)
     xr[x_me * 8 + p_me] = xo[p_me, x_me]
 
     hear(1)
@@ -338,18 +333,15 @@
     left = dot(occ_both, forms[y_me], ((0,), (0,))).astype(BF16)
     z_tiles = dot(put, to_tiles(dot(left, vir[...])).astype(BF16))
     zo[...] = z_tiles.reshape(8, 8, 1024).astype(BF16)
-    z_copies = exchange(by_pair, 8, lambda q: zo.at[q], zt.at[f_me], s_z, r_z)
-    started += z_copies
+    exchange(by_pair, 8, lambda q: zo.at[q], zt.at[f_me], s_z, r_z)
     zt[f_me] = zo[p_me]
 
-    for c in x_copies:
-        c.wait_recv()
+    await_all(xr.at[pl.ds(0, 31)], r_x)
     ar[z_me] = jnp.sum(xr[...].astype(F32), axis=0).astype(BF16)
     hear(2)
-    a_copies = exchange(by_z, NZ, lambda z: ar.at[z_me], ar.at[z_me], s_a, r_a)
-
-    for c in z_copies:
-        c.wait_recv()
+    exchange(by_z, NZ, lambda z: ar.at[z_me], ar.at[z_me], s_a, r_a)
+
+    await_all(zt.at[pl.ds(0, 7)], r_z)
     z_rows = rows64(zt[...]).astype(BF16)
     chi_total = jnp.zeros((8, 128), F32)
     for slot in range(5):
@@ -361,29 +353,27 @@
         gather = jnp.where(iota((64, 128), 1) == slot * 8 + iota((64, 128), 0) // 8, 1.0, 0.0)
         chi_total += jnp.dot(terms, gather, precision=lax.Precision.HIGHEST, preferred_element_type=F32)
     chi[p_me] = chi_total * (1.0 / (OA * NAT))
-    c_copies = exchange(by_pair, 8, lambda q: chi.at[p_me], chi.at[p_me], s_c, r_c)
-    started += c_copies
-
-    for c in started + x_copies:
-        c.wait_send()
-    for c in a_copies:
-        c.wait_recv()
+    exchange(by_pair, 8, lambda q: chi.at[p_me], chi.at[p_me], s_c, r_c)
+
+    await_all(win.at[pl.ds(0, 4)], s_win)
+    await_all(mt.at[pl.ds(0, 7)], s_m)
+    v_copy.wait_send()
+    await_all(zt.at[pl.ds(0, 7)], s_z)
+    await_all(xr.at[pl.ds(0, 31)], s_x)
+    await_all(ar.at[pl.ds(0, NZ - 1)], r_a)
     scale = -1.0 / math.sqrt(n_aux * 8 * NAT * OA * NAT)
     fin[x_me] = jnp.sum(ar[...].astype(F32), axis=0) * scale
-    f_copies = exchange(by_x, NX, lambda x: fin.at[x_me], fin.at[x_me], s_f, r_f)
-
-    for c in c_copies:
-        c.wait_recv()
+    exchange(by_x, NX, lambda x: fin.at[x_me], fin.at[x_me], s_f, r_f)
+
+    await_all(chi.at[pl.ds(0, 7)], r_c)
     turned = pltpu.roll(jnp.sum(chi[...], axis=0), lax.rem(128 - 5 * p_me, 128), 1)
     pol_ref[...] = turned[:, :5]
-    for c in a_copies:
-        c.wait_send()
-    for c in f_copies:
-        c.wait_recv()
+    await_all(ar.at[pl.ds(0, NZ - 1)], s_a)
+    await_all(chi.at[pl.ds(0, 7)], s_c)
+    await_all(fin.at[pl.ds(0, NX - 1)], r_f)
     for x in range(NX):
         self_ref[:, x * 256 : (x + 1) * 256] = fin[x]
-    for c in f_copies:
-        c.wait_send()
+    await_all(fin.at[pl.ds(0, NX - 1)], s_f)
 
 
 def solution(mesh):
@@ -391,7 +381,6 @@
 
     def per_device(three_center, tile_live, pair_atoms, green_occ, green_vir, screened):
         tiles = pltpu.VMEM((8, 8, 1024), BF16)
-        sems = pltpu.SemaphoreType.DMA((7,))
         return pl.pallas_call(
             functools.partial(kernel, n_aux, n_pair),
             out_shape=(
@@ -420,13 +409,10 @@
                 pltpu.VMEM((NZ, 8, 256), BF16),
                 pltpu.VMEM((NX, 8, 256), F32),
                 pltpu.SemaphoreType.DMA((6,)),
-                *[pltpu.SemaphoreType.DMA((2, 4))] * 4,
-                *[sems] * 4,
-                *[pltpu.SemaphoreType.DMA(())] * 2,
-                *[pltpu.SemaphoreType.DMA((31,))] * 2,
-                *[sems] * 2,
-                *[pltpu.SemaphoreType.DMA((15,))] * 2,
-                *[sems] * 2,
+                pltpu.SemaphoreType.DMA(()),
+                pltpu.SemaphoreType.DMA((2, 4)),
+                pltpu.SemaphoreType.DMA((2,)),
+                *[pltpu.SemaphoreType.DMA(())] * 14,
                 pltpu.SemaphoreType.REGULAR((3,)),
             ],
             compiler_params=pltpu.CompilerParams(

time: 44.5 us -> 41.9 us (0.942)
  Pallas kernels: 42.5 us -> 39.9 us
    pallas_call x1, Pallas kernels: 42.5 us -> 39.9 us  [per_device(): pl.pallas_call(functools.partial(kernel, n_aux, n_pair), out_shape=(jax.S...]
where the time goes in v6:
time: 41.9 us; the launch traced here: 41.7 us
  Pallas kernels  39.9 us (95%)
  local copies, waits for them, and re-layouts  1.21 us (3%)
  between operations  0.64 us (2%)
    pallas_call x1, Pallas kernels, per_device(): pl.pallas_call(functools.partial(kernel, n_aux, n_pair), out_shape=(jax.S...  39.9 us
    unnamed x2, local copies, waits for them, and re-layouts  1.21 us

profile of v6, /device:TPU:1, one launch (start us, length us, event | category | flops | bytes accessed | tf_op | source)
XLA Modules:
  0.0 41.7 jit_solution(7590627998115190670)
XLA Ops:
  0.6 39.9 %shard_map.77 = (f32[8,5]{1,0:T(8,128)S(1)}, f32[8,1024]{1,0:T(8,128)S(1)}) custom-call(bf16[8,8,1024]{2,1,0:T(8,128)(2,1)} %tc_hbm.1, s32[1,8]{1,0:T(1,128)} %live_hbm.1, s32[1,64]{1,0:T(1,128)} %bitcast.1, bf16[256,256]{1,0:T(8,128)(2,1)} %occ_hbm.1, bf16[256,256]{1,0:T(8,128)(2,1)} %vir_hbm.1, bf16[8,40]{1,0:T(8,128)(2,1)} %scr_hbm.1), custom_call_target="tpu_custom_call" | custom-call | tf_op jit(solution)/shard_map/pallas_call | solution.py:384
  40.5 0.6 %copy.10 = f32[8,5]{1,0:T(8,128)} copy(f32[8,5]{1,0:T(8,128)S(1)} %get-tuple-element.4) | data formatting | bytes 320
  41.1 0.6 %copy.11 = f32[8,1024]{1,0:T(8,128)} copy(f32[8,1024]{1,0:T(8,128)S(1)} %get-tuple-element.5) | data formatting | bytes 65536

commit v7 on v6

--- a/solution.py
+++ b/solution.py
@@ -127,6 +127,37 @@
     y_me, c_me = p_me // 2, p_me % 2
     f_me = c_me * 4 + y_me
 
+    def by_pair(step):
+        q = lax.rem(p_me + step, n_pair)
+        return q, (a_me, q)
+
+    def by_plane(step):
+        q = lax.rem(p_me + step % 8, n_pair)
+        x = lax.rem(x_me + step // 8, NX)
+        return q, x, (x * NZ + z_me, q)
+
+    def by_z(step):
+        z = lax.rem(z_me + step, NZ)
+        return z, (x_me * NZ + z, p_me)
+
+    def by_x(step):
+        x = lax.rem(x_me + step, NX)
+        return x, (x * NZ + z_me, p_me)
+
+    offsets = (1, -1)
+    chunks = [pl.ds(2 * c, 2) for c in range(4)]
+
+    def by_window(d):
+        return (lax.rem(a_me + d + n_aux, n_aux), p_me)
+
+    barrier = pltpu.get_barrier_semaphore()
+    peers = [by_window(d) for d in offsets]
+    peers += [by_x(step)[-1] for step in (2, 1, 3)]
+    peers += [by_pair(step)[-1] for step in range(1, 8)]
+    peers += [by_z(step)[-1] for step in (1, NZ - 1)]
+    for device in peers:
+        pl.semaphore_signal(barrier, inc=1, device_id=device, device_id_type=MESH)
+
     loads = [
         pltpu.make_async_copy(src, dst, in_sem.at[i])
         for i, (src, dst) in enumerate(
@@ -143,37 +174,6 @@
     for c in loads:
         c.start()
 
-    def by_pair(step):
-        q = lax.rem(p_me + step, n_pair)
-        return q, (a_me, q)
-
-    def by_plane(step):
-        q = lax.rem(p_me + step % 8, n_pair)
-        x = lax.rem(x_me + step // 8, NX)
-        return q, x, (x * NZ + z_me, q)
-
-    def by_z(step):
-        z = lax.rem(z_me + step, NZ)
-        return z, (x_me * NZ + z, p_me)
-
-    def by_x(step):
-        x = lax.rem(x_me + step, NX)
-        return x, (x * NZ + z_me, p_me)
-
-    offsets = (1, -1)
-    chunks = [pl.ds(2 * c, 2) for c in range(4)]
-
-    def by_window(d):
-        return (lax.rem(a_me + d + n_aux, n_aux), p_me)
-
-    barrier = pltpu.get_barrier_semaphore()
-    peers = [by_window(d) for d in offsets]
-    peers += [by_x(step)[-1] for step in (2, 1, 3)]
-    peers += [by_pair(step)[-1] for step in range(1, 8)]
-    peers += [by_z(step)[-1] for step in (1, NZ - 1)]
-    for device in peers:
-        pl.semaphore_signal(barrier, inc=1, device_id=device, device_id_type=MESH)
-
     def tell(r):
         for step in (1 << r, NZ - (1 << r)):
             pl.semaphore_signal(known.at[r], inc=1, device_id=by_z(step)[-1], device_id_type=MESH)
@@ -221,10 +221,16 @@
             )
             copy.start()
             arriving[REACH - d].append(copy)
-    exchange(
-        by_pair, 8, lambda q: win.at[REACH, pl.ds(4 * (q % 2), 4)], mt.at[p_me], s_m, r_m
-    )
-    mt[p_me] = win[REACH, pl.ds(4 * c_me, 4)]
+    for h in range(2):
+        exchange(
+            by_pair,
+            8,
+            lambda q: win.at[REACH, pl.ds(4 * (q % 2) + 2 * h, 2)],
+            mt.at[h, p_me],
+            s_m,
+            r_m.at[h],
+        )
+        mt[h, p_me] = win[REACH, pl.ds(4 * c_me + 2 * h, 2)]
 
     for c in loads[2:]:
         c.wait()
@@ -290,8 +296,17 @@
     hear(0)
     tell(1)
 
+    def n_half(h):
+        await_all(mt.at[h, pl.ds(0, 7)], r_m.at[h])
+        for i in range(2):
+            form = to_matrix(dot(pick, rows64(mt[h, :, i]).astype(BF16))).astype(BF16)
+            forms[2 * h + i] = form
+            near[:, 2 * h + i] = dot(occ_cols, form).reshape(NAT, OA, 256).astype(BF16)
+
     mixed = dot(couple[2], rows64(win[2]).astype(BF16))
     for slot in (1, 3, 0, 4):
+        if slot == 0:
+            n_half(0)
         if slot in (0, 4):
             await_all(win.at[slot], r_far.at[slot // 4])
         mixed += dot(couple[slot], rows64(win[slot]).astype(BF16))
@@ -302,11 +317,7 @@
     v_copy.start()
     vt[c_me] = vo[pl.ds(4 * c_me, 4)]
 
-    await_all(mt.at[pl.ds(0, 7)], r_m)
-    for i in range(4):
-        form = to_matrix(dot(pick, rows64(mt[:, i]).astype(BF16))).astype(BF16)
-        forms[i] = form
-        near[:, i] = dot(occ_cols, form).reshape(NAT, OA, 256).astype(BF16)
+    n_half(1)
 
     v_copy.wait_recv()
     v_form = to_matrix(rows64(vt[...]))
@@ -356,7 +367,7 @@
     exchange(by_pair, 8, lambda q: chi.at[p_me], chi.at[p_me], s_c, r_c)
 
     await_all(win.at[pl.ds(0, 4)], s_win)
-    await_all(mt.at[pl.ds(0, 7)], s_m)
+    await_all(mt.at[:, pl.ds(0, 7)], s_m)
     v_copy.wait_send()
     await_all(zt.at[pl.ds(0, 7)], s_z)
     await_all(xr.at[pl.ds(0, 31)], s_x)
@@ -397,7 +408,7 @@
                 pltpu.VMEM((256, 256), BF16),
                 pltpu.VMEM((8, 40), BF16),
                 pltpu.VMEM((5, 8, 8, 1024), BF16),
-                pltpu.VMEM((8, 4, 8, 1024), BF16),
+                pltpu.VMEM((2, 8, 2, 8, 1024), BF16),
                 *[tiles] * 3,
                 pltpu.VMEM((2, 4, 8, 1024), BF16),
                 pltpu.VMEM((64, 128), jnp.int32),
@@ -412,7 +423,9 @@
                 pltpu.SemaphoreType.DMA(()),
                 pltpu.SemaphoreType.DMA((2, 4)),
                 pltpu.SemaphoreType.DMA((2,)),
-                *[pltpu.SemaphoreType.DMA(())] * 14,
+                pltpu.SemaphoreType.DMA(()),
+                pltpu.SemaphoreType.DMA((2,)),
+                *[pltpu.SemaphoreType.DMA(())] * 12,
                 pltpu.SemaphoreType.REGULAR((3,)),
             ],
             compiler_params=pltpu.CompilerParams(

time: 41.9 us -> 41.4 us (0.988)
  Pallas kernels: 39.9 us -> 39.2 us
    pallas_call x1, Pallas kernels: 39.9 us -> 39.2 us  [per_device(): pl.pallas_call(functools.partial(kernel, n_aux, n_pair), out_shape=(jax.S...]
where the time goes in v7:
time: 41.4 us; the launch traced here: 41 us
  Pallas kernels  39.2 us (95%)
  local copies, waits for them, and re-layouts  1.21 us (3%)
  between operations  0.64 us (2%)
    pallas_call x1, Pallas kernels, per_device(): pl.pallas_call(functools.partial(kernel, n_aux, n_pair), out_shape=(jax.S...  39.2 us
    unnamed x2, local copies, waits for them, and re-layouts  1.21 us

profile of v7, /device:TPU:1, one launch (start us, length us, event | category | flops | bytes accessed | tf_op | source)
XLA Modules:
  0.0 41.0 jit_solution(17618935187611351455)
XLA Ops:
  0.6 39.2 %shard_map.77 = (f32[8,5]{1,0:T(8,128)S(1)}, f32[8,1024]{1,0:T(8,128)S(1)}) custom-call(bf16[8,8,1024]{2,1,0:T(8,128)(2,1)} %tc_hbm.1, s32[1,8]{1,0:T(1,128)} %live_hbm.1, s32[1,64]{1,0:T(1,128)} %bitcast.1, bf16[256,256]{1,0:T(8,128)(2,1)} %occ_hbm.1, bf16[256,256]{1,0:T(8,128)(2,1)} %vir_hbm.1, bf16[8,40]{1,0:T(8,128)(2,1)} %scr_hbm.1), custom_call_target="tpu_custom_call" | custom-call | tf_op jit(solution)/shard_map/pallas_call | solution.py:395
  39.8 0.6 %copy.10 = f32[8,5]{1,0:T(8,128)} copy(f32[8,5]{1,0:T(8,128)S(1)} %get-tuple-element.4) | data formatting | bytes 320
  40.4 0.6 %copy.11 = f32[8,1024]{1,0:T(8,128)} copy(f32[8,1024]{1,0:T(8,128)S(1)} %get-tuple-element.5) | data formatting | bytes 65536

commit v8 on v7

--- a/solution.py
+++ b/solution.py
@@ -100,6 +100,7 @@
     xr,
     chi,
     ar,
+    both,
     fin,
     in_sem,
     s_win,
@@ -131,10 +132,10 @@
         q = lax.rem(p_me + step, n_pair)
         return q, (a_me, q)
 
-    def by_plane(step):
-        q = lax.rem(p_me + step % 8, n_pair)
-        x = lax.rem(x_me + step // 8, NX)
-        return q, x, (x * NZ + z_me, q)
+    def by_chip(step):
+        x = lax.rem(x_me + step // 4, NX)
+        y = lax.rem(y_me + step % 4, 4)
+        return y, x, (x * NZ + z_me, y * 2 + 1)
 
     def by_z(step):
         z = lax.rem(z_me + step, NZ)
@@ -197,9 +198,7 @@
             remote(source(*there), dest, send, recv, device).start()
 
     def distance(peer, step):
-        if peer is by_plane:
-            return abs(step % 8 - 4) + 2 * abs(step // 8 - 2)
-        return abs(step - {by_pair: 4, by_z: NZ // 2, by_x: 2}[peer])
+        return abs(step - {by_pair: 4, by_z: NZ // 2}[peer])
 
     def await_all(slots, sem):
         pltpu.make_async_copy(slots, slots, sem).wait()
@@ -335,9 +334,19 @@
     lower = [(v - u.astype(F32)).astype(BF16) for v, u in zip(blocks, upper)]
     energy_tiles = dot(collect, jnp.concatenate(upper + lower, axis=0))
     for x in range(NX):
-        xo[:, x] = energy_tiles[:, x * 256 : (x + 1) * 256].reshape(8, 8, 256).astype(BF16)
-    exchange(by_plane, 32, lambda q, x: xo.at[q, x], xr.at[x_me * 8 + p_me], s_x, r_x)
-    xr[x_me * 8 + p_me] = xo[p_me, x_me]
+        xo[:, x] = energy_tiles[:, x * 256 : (x + 1) * 256].reshape(4, 2, 8, 256).astype(BF16)
+    sender = x_me * 8 + p_me
+    for step in sorted(range(1, 16), key=lambda v: abs(v % 4 - 2) + abs(v // 4 - 2)):
+        y, x, device = by_chip(step)
+        remote(xo.at[y, x], xr.at[sender], s_x, r_x, device).start()
+
+    @pl.when(c_me == 0)
+    def _():
+        remote(xo.at[y_me, x_me], xr.at[sender], s_x, r_x, by_chip(0)[-1]).start()
+
+    @pl.when(c_me == 1)
+    def _():
+        xr[sender] = xo[y_me, x_me]
 
     hear(1)
     tell(2)
@@ -347,10 +356,15 @@
     exchange(by_pair, 8, lambda q: zo.at[q], zt.at[f_me], s_z, r_z)
     zt[f_me] = zo[p_me]
 
-    await_all(xr.at[pl.ds(0, 31)], r_x)
-    ar[z_me] = jnp.sum(xr[...].astype(F32), axis=0).astype(BF16)
     hear(2)
-    exchange(by_z, NZ, lambda z: ar.at[z_me], ar.at[z_me], s_a, r_a)
+
+    @pl.when(c_me == 1)
+    def _():
+        await_all(xr.at[pl.ds(0, 31)], r_x)
+        for core in (1, 0):
+            ar[core, z_me] = jnp.sum(xr[:, core].astype(F32), axis=0).astype(BF16)
+            own = ar.at[core, z_me]
+            exchange(by_z, NZ, lambda z: own, own, s_a.at[core], r_a.at[core])
 
     await_all(zt.at[pl.ds(0, 7)], r_z)
     z_rows = rows64(zt[...]).astype(BF16)
@@ -370,21 +384,48 @@
     await_all(mt.at[:, pl.ds(0, 7)], s_m)
     v_copy.wait_send()
     await_all(zt.at[pl.ds(0, 7)], s_z)
-    await_all(xr.at[pl.ds(0, 31)], s_x)
-    await_all(ar.at[pl.ds(0, NZ - 1)], r_a)
+    @pl.when(c_me == 0)
+    def _():
+        await_all(xr.at[pl.ds(0, 16)], s_x)
+
+    @pl.when(c_me == 1)
+    def _():
+        await_all(xr.at[pl.ds(0, 15)], s_x)
+
     scale = -1.0 / math.sqrt(n_aux * 8 * NAT * OA * NAT)
-    fin[x_me] = jnp.sum(ar[...].astype(F32), axis=0) * scale
-    exchange(by_x, NX, lambda x: fin.at[x_me], fin.at[x_me], s_f, r_f)
+
+    @pl.when(c_me == 1)
+    def _():
+        for core in (1, 0):
+            await_all(ar.at[core, pl.ds(0, NZ - 1)], r_a.at[core])
+            both[core] = jnp.sum(ar[core].astype(F32), axis=0) * scale
+            for step in (2, 1, 3):
+                there = (by_x(step)[-1][0], y_me * 2 + core)
+                remote(both.at[core], fin.at[x_me], s_f, r_f, there).start()
+        remote(both.at[0], fin.at[x_me], s_f, r_f, (a_me, y_me * 2)).start()
+        fin[x_me] = both[1]
 
     await_all(chi.at[pl.ds(0, 7)], r_c)
     turned = pltpu.roll(jnp.sum(chi[...], axis=0), lax.rem(128 - 5 * p_me, 128), 1)
     pol_ref[...] = turned[:, :5]
-    await_all(ar.at[pl.ds(0, NZ - 1)], s_a)
     await_all(chi.at[pl.ds(0, 7)], s_c)
-    await_all(fin.at[pl.ds(0, NX - 1)], r_f)
+
+    @pl.when(c_me == 1)
+    def _():
+        for core in range(2):
+            await_all(ar.at[core, pl.ds(0, NZ - 1)], s_a.at[core])
+        await_all(fin.at[pl.ds(0, NX - 1)], r_f)
+
+    @pl.when(c_me == 0)
+    def _():
+        await_all(fin, r_f)
+
     for x in range(NX):
         self_ref[:, x * 256 : (x + 1) * 256] = fin[x]
-    await_all(fin.at[pl.ds(0, NX - 1)], s_f)
+
+    @pl.when(c_me == 1)
+    def _():
+        await_all(xr.at[pl.ds(0, 7)], s_f)
 
 
 def solution(mesh):
@@ -414,10 +455,11 @@
                 pltpu.VMEM((64, 128), jnp.int32),
                 pltpu.VMEM((4, 256, 256), BF16),
                 pltpu.VMEM((NAT, 4, OA, 256), BF16),
-                pltpu.VMEM((8, NX, 8, 256), BF16),
-                pltpu.VMEM((32, 8, 256), BF16),
+                pltpu.VMEM((4, NX, 2, 8, 256), BF16),
+                pltpu.VMEM((32, 2, 8, 256), BF16),
                 pltpu.VMEM((8, 8, 128), F32),
-                pltpu.VMEM((NZ, 8, 256), BF16),
+                pltpu.VMEM((2, NZ, 8, 256), BF16),
+                pltpu.VMEM((2, 8, 256), F32),
                 pltpu.VMEM((NX, 8, 256), F32),
                 pltpu.SemaphoreType.DMA((6,)),
                 pltpu.SemaphoreType.DMA(()),
@@ -425,7 +467,9 @@
                 pltpu.SemaphoreType.DMA((2,)),
                 pltpu.SemaphoreType.DMA(()),
                 pltpu.SemaphoreType.DMA((2,)),
-                *[pltpu.SemaphoreType.DMA(())] * 12,
+                *[pltpu.SemaphoreType.DMA(())] * 8,
+                *[pltpu.SemaphoreType.DMA((2,))] * 2,
+                *[pltpu.SemaphoreType.DMA(())] * 2,
                 pltpu.SemaphoreType.REGULAR((3,)),
             ],
             compiler_params=pltpu.CompilerParams(

time: 41.4 us -> 41.2 us (level)
  no operation moved by 1% of the time
where the time goes in v8:
time: 41.2 us; the launch traced here: 41.1 us
  Pallas kernels  39.3 us (95%)
  local copies, waits for them, and re-layouts  1.21 us (3%)
  between operations  0.64 us (2%)
    pallas_call x1, Pallas kernels, per_device(): pl.pallas_call(functools.partial(kernel, n_aux, n_pair), out_shape=(jax.S...  39.3 us
    unnamed x2, local copies, waits for them, and re-layouts  1.21 us

profile of v8, /device:TPU:1, one launch (start us, length us, event | category | flops | bytes accessed | tf_op | source)
XLA Modules:
  0.0 41.1 jit_solution(14402851164551270804)
XLA Ops:
  0.6 39.3 %shard_map.77 = (f32[8,5]{1,0:T(8,128)S(1)}, f32[8,1024]{1,0:T(8,128)S(1)}) custom-call(bf16[8,8,1024]{2,1,0:T(8,128)(2,1)} %tc_hbm.1, s32[1,8]{1,0:T(1,128)} %live_hbm.1, s32[1,64]{1,0:T(1,128)} %bitcast.1, bf16[256,256]{1,0:T(8,128)(2,1)} %occ_hbm.1, bf16[256,256]{1,0:T(8,128)(2,1)} %vir_hbm.1, bf16[8,40]{1,0:T(8,128)(2,1)} %scr_hbm.1), custom_call_target="tpu_custom_call" | custom-call | tf_op jit(solution)/shard_map/pallas_call | solution.py:436
  39.9 0.6 %copy.10 = f32[8,5]{1,0:T(8,128)} copy(f32[8,5]{1,0:T(8,128)S(1)} %get-tuple-element.4) | data formatting | bytes 320
  40.5 0.6 %copy.11 = f32[8,1024]{1,0:T(8,128)} copy(f32[8,1024]{1,0:T(8,128)S(1)} %get-tuple-element.5) | data formatting | bytes 65536

commit v9 on v8

--- a/solution.py
+++ b/solution.py
@@ -103,8 +103,9 @@
     both,
     fin,
     in_sem,
-    s_win,
-    r_win,
+    s_near,
+    r_near,
+    s_far,
     r_far,
     s_m,
     r_m,
@@ -148,6 +149,9 @@
     offsets = (1, -1)
     chunks = [pl.ds(2 * c, 2) for c in range(4)]
 
+    def inside(block):
+        return jnp.logical_and(block >= 0, block < n_aux)
+
     def by_window(d):
         return (lax.rem(a_me + d + n_aux, n_aux), p_me)
 
@@ -211,15 +215,30 @@
     )
     win[REACH] = (tc[...].astype(F32) * live_col[None]).astype(BF16)
 
+    for slot in (0, 1, 3, 4):
+
+        @pl.when(jnp.logical_not(inside(a_me + slot - REACH)))
+        def _():
+            win[slot] = jnp.zeros((8, 8, 1024), BF16)
+
     pl.semaphore_wait(barrier, len(peers))
-    arriving = {1: [], 3: []}
-    for c, part in enumerate(chunks):
+    def near_copy(i, c):
+        slot = REACH - offsets[i]
+        return remote(
+            win.at[REACH, chunks[c]],
+            win.at[slot, chunks[c]],
+            s_near.at[i],
+            r_near.at[i, c],
+            by_window(offsets[i]),
+        )
+
+    for c in range(len(chunks)):
         for i, d in enumerate(offsets):
-            copy = remote(
-                win.at[REACH, part], win.at[REACH - d, part], s_win, r_win.at[i, c], by_window(d)
-            )
-            copy.start()
-            arriving[REACH - d].append(copy)
+
+            @pl.when(inside(a_me + d))
+            def _():
+                near_copy(i, c).start()
+
     for h in range(2):
         exchange(
             by_pair,
@@ -275,23 +294,27 @@
     couple = []
     for slot in range(5):
         spread = jnp.where(iota((40, 64), 0) == slot * 8 + iota((40, 64), 1) // 8, 1.0, 0.0)
-        block = a_me + slot - REACH
-        inside = jnp.logical_and(block >= 0, block < n_aux)
-        keep = jnp.logical_and(same_tile, inside)
+        keep = jnp.logical_and(same_tile, inside(a_me + slot - REACH))
         couple.append(jnp.where(keep, dot(wide, spread.astype(BF16)), 0.0).astype(BF16))
 
     tell(0)
     for c, part in enumerate(chunks):
         for i, d in enumerate(offsets):
-            arriving[REACH - d][c].wait_recv()
-            copy = remote(
-                win.at[REACH - d, part],
-                win.at[REACH - 2 * d, part],
-                s_win,
-                r_far.at[i],
-                by_window(d),
-            )
-            copy.start()
+
+            @pl.when(inside(a_me - d))
+            def _():
+                near_copy(i, c).wait_recv()
+
+            @pl.when(jnp.logical_and(inside(a_me - d), inside(a_me + d)))
+            def _():
+                remote(
+                    win.at[REACH - d, part],
+                    win.at[REACH - 2 * d, part],
+                    s_far.at[i],
+                    r_far.at[i],
+                    by_window(d),
+                ).start()
+
     hear(0)
     tell(1)
 
@@ -307,7 +330,11 @@
         if slot == 0:
             n_half(0)
         if slot in (0, 4):
-            await_all(win.at[slot], r_far.at[slot // 4])
+
+            @pl.when(inside(a_me + slot - REACH))
+            def _():
+                await_all(win.at[slot], r_far.at[slot // 4])
+
         mixed += dot(couple[slot], rows64(win[slot]).astype(BF16))
     vo[...] = mixed.reshape(8, 8, 1024).astype(BF16)
     v_copy = remote(
@@ -371,16 +398,23 @@
     chi_total = jnp.zeros((8, 128), F32)
     for slot in range(5):
         terms = dot(z_rows, rows64(win[slot]).astype(BF16), ((1,), (1,)))
-        block = a_me + slot - REACH
-        inside = jnp.logical_and(block >= 0, block < n_aux)
-        keep = jnp.logical_and(same_tile, inside)
+        keep = jnp.logical_and(same_tile, inside(a_me + slot - REACH))
         terms = jnp.sum(jnp.where(keep, terms, 0.0).reshape(8, 8, 64), axis=1)
         gather = jnp.where(iota((64, 128), 1) == slot * 8 + iota((64, 128), 0) // 8, 1.0, 0.0)
         chi_total += jnp.dot(terms, gather, precision=lax.Precision.HIGHEST, preferred_element_type=F32)
     chi[p_me] = chi_total * (1.0 / (OA * NAT))
     exchange(by_pair, 8, lambda q: chi.at[p_me], chi.at[p_me], s_c, r_c)
 
-    await_all(win.at[pl.ds(0, 4)], s_win)
+    for i, d in enumerate(offsets):
+
+        @pl.when(inside(a_me + d))
+        def _():
+            await_all(win.at[REACH], s_near.at[i])
+
+        @pl.when(jnp.logical_and(inside(a_me - d), inside(a_me + d)))
+        def _():
+            await_all(win.at[REACH], s_far.at[i])
+
     await_all(mt.at[:, pl.ds(0, 7)], s_m)
     v_copy.wait_send()
     await_all(zt.at[pl.ds(0, 7)], s_z)
@@ -462,9 +496,9 @@
                 pltpu.VMEM((2, 8, 256), F32),
                 pltpu.VMEM((NX, 8, 256), F32),
                 pltpu.SemaphoreType.DMA((6,)),
-                pltpu.SemaphoreType.DMA(()),
+                pltpu.SemaphoreType.DMA((2,)),
                 pltpu.SemaphoreType.DMA((2, 4)),
-                pltpu.SemaphoreType.DMA((2,)),
+                *[pltpu.SemaphoreType.DMA((2,))] * 2,
                 pltpu.SemaphoreType.DMA(()),
                 pltpu.SemaphoreType.DMA((2,)),
                 *[pltpu.SemaphoreType.DMA(())] * 8,

time: 41.2 us -> 41.2 us (level)
  no operation moved by 1% of the time
where the time goes in v9:
time: 41.2 us; the launch traced here: 41.1 us
  Pallas kernels  39.2 us (95%)
  local copies, waits for them, and re-layouts  1.21 us (3%)
  between operations  0.64 us (2%)
    pallas_call x1, Pallas kernels, per_device(): pl.pallas_call(functools.partial(kernel, n_aux, n_pair), out_shape=(jax.S...  39.2 us
    unnamed x2, local copies, waits for them, and re-layouts  1.21 us

profile of v9, /device:TPU:1, one launch (start us, length us, event | category | flops | bytes accessed | tf_op | source)
XLA Modules:
  0.0 41.1 jit_solution(3100308454553576836)
XLA Ops:
  0.6 39.2 %shard_map.77 = (f32[8,5]{1,0:T(8,128)S(1)}, f32[8,1024]{1,0:T(8,128)S(1)}) custom-call(bf16[8,8,1024]{2,1,0:T(8,128)(2,1)} %tc_hbm.1, s32[1,8]{1,0:T(1,128)} %live_hbm.1, s32[1,64]{1,0:T(1,128)} %bitcast.1, bf16[256,256]{1,0:T(8,128)(2,1)} %occ_hbm.1, bf16[256,256]{1,0:T(8,128)(2,1)} %vir_hbm.1, bf16[8,40]{1,0:T(8,128)(2,1)} %scr_hbm.1), custom_call_target="tpu_custom_call" | custom-call | tf_op jit(solution)/shard_map/pallas_call | solution.py:470
  39.9 0.6 %copy.10 = f32[8,5]{1,0:T(8,128)} copy(f32[8,5]{1,0:T(8,128)S(1)} %get-tuple-element.4) | data formatting | bytes 320
  40.5 0.6 %copy.11 = f32[8,1024]{1,0:T(8,128)} copy(f32[8,1024]{1,0:T(8,128)S(1)} %get-tuple-element.5) | data formatting | bytes 65536
